TPU v7x, 32 devices: a whole 2x2x4 slice. The times are simulated.
32 devices in a mesh: section: 8 (over y, x, core), dp: 4 (over z).
Axes of the slice: x: 2, y: 2, z: 4, core: 2. Of those that a mesh axis runs over, the one named last changes fastest.
Arguments:
- feed: bfloat16 [2, 4, 64, 512], P(None, None, 'dp'), may hold values from -6 to 6
- proj_in: bfloat16 [2, 8, 512, 1536], P(None, 'section'), may hold values from -0.25 to 0.25
- proj_out: bfloat16 [2, 8, 1536, 512], P(None, 'section'), may hold values from -0.15625 to 0.15625
Outputs:
- grad_a: float32 [8, 512, 1536], P('section', 'dp')
- grad_b: float32 [8, 1536, 512], P('section', 'dp')
All inputs are finite; a program needn't handle non-finite values.
Results may differ from a plain program's by a relative error of at most 0.023.
Values may be sent and summed in bfloat16 or wider, within the bound.
A program may use at most 64 MiB of HBM per device.

v0:
```python
import jax
import jax.numpy as jnp
from jax import lax
from jax.sharding import PartitionSpec as P


def shifted(value, axis, steps):
    count = lax.axis_size(axis)
    first, last = (max(0, -steps), min(count, count - steps))
    return lax.ppermute(value, axis, [(source, source + steps) for source in range(first, last)])


def forward_section(activ, weight_in, weight_out):
    wide = activ.astype(jnp.float32)
    factor = lax.rsqrt(jnp.mean(wide * wide, axis=-1, keepdims=True) + 1e-05)
    normed = (wide * factor).astype(jnp.bfloat16)
    before = jnp.dot(normed, weight_in, preferred_element_type=jnp.float32)
    hidden = (before * jax.nn.sigmoid(before)).astype(jnp.bfloat16)
    result = (wide + jnp.dot(hidden, weight_out, preferred_element_type=jnp.float32)).astype(
        jnp.bfloat16
    )
    return (result, before)


def backward_section(activ, before, weight_in, weight_out, incoming):
    wide = activ.astype(jnp.float32)
    factor = lax.rsqrt(jnp.mean(wide * wide, axis=-1, keepdims=True) + 1e-05)
    scaled = wide * factor
    d_hidden = jnp.einsum("md,rd->mr", incoming, weight_out, preferred_element_type=jnp.float32)
    sigma = jax.nn.sigmoid(before)
    d_before = (d_hidden * sigma * (1.0 + before * (1.0 - sigma))).astype(jnp.bfloat16)
    d_normed = jnp.einsum("mr,dr->md", d_before, weight_in, preferred_element_type=jnp.float32)
    outgoing = incoming.astype(jnp.float32) + factor * (
        d_normed - scaled * jnp.mean(d_normed * scaled, axis=-1, keepdims=True)
    )
    return (outgoing.astype(jnp.bfloat16), d_before)


def weight_terms(kept, befores, seeds, d_befores):
    wide = kept.astype(jnp.float32)
    factor = lax.rsqrt(jnp.mean(wide * wide, axis=-1, keepdims=True) + 1e-05)
    normed = (wide * factor).astype(jnp.bfloat16)
    hidden = (befores * jax.nn.sigmoid(befores)).astype(jnp.bfloat16)
    term_in = jnp.einsum("jmd,jmr->dr", normed, d_befores, preferred_element_type=jnp.float32)
    term_out = jnp.einsum("jmr,jmd->rd", hidden, seeds, preferred_element_type=jnp.float32)
    return (term_in, term_out)


def read_slot(buffer, index):
    return lax.dynamic_index_in_dim(buffer, index, 0, keepdims=False)


def store_slot(buffer, index, value, valid):
    old_value = read_slot(buffer, index)
    return lax.dynamic_update_index_in_dim(buffer, jnp.where(valid, value, old_value), index, 0)


def per_device(feed, proj_in, proj_out):
    section_count = lax.axis_size("section")
    position = lax.axis_index("section")
    replica_count = lax.axis_size("dp")
    micro_count, row_count, feature_count = (feed.shape[1], feed.shape[2], feed.shape[3])
    in_down, in_up = (proj_in[0, 0], proj_in[1, 0])
    out_down, out_up = (proj_out[0, 0], proj_out[1, 0])
    unit_count = in_down.shape[1]
    final_section = section_count - 1
    tick_count = micro_count + final_section
    seed_scale = 8.0 / (micro_count * row_count * replica_count)
    blank_rows = jnp.zeros((row_count, feature_count), jnp.bfloat16)
    blank_acts = jnp.zeros((micro_count, row_count, feature_count), jnp.bfloat16)
    blank_units = jnp.zeros((micro_count, row_count, unit_count), jnp.float32)
    blank_grads = jnp.zeros((micro_count, row_count, unit_count), jnp.bfloat16)

    def slot_of(step_index, offset):
        slot = step_index - offset
        live = (slot >= 0) & (slot < micro_count)
        return (jnp.clip(slot, 0, micro_count - 1), live)

    def forward_tick(step_index, state):
        from_left, from_right, kept_down, kept_up, pre_down, pre_up, last_down, last_up = state
        index_down, live_down = slot_of(step_index, position)
        index_up, live_up = slot_of(step_index, final_section - position)
        act_down = jnp.where(position == 0, read_slot(feed[0], index_down), from_left)
        act_up = jnp.where(position == final_section, read_slot(feed[1], index_up), from_right)
        next_down, before_down = forward_section(act_down, in_down, out_down)
        next_up, before_up = forward_section(act_up, in_up, out_up)
        kept_down = store_slot(kept_down, index_down, act_down, live_down)
        kept_up = store_slot(kept_up, index_up, act_up, live_up)
        pre_down = store_slot(pre_down, index_down, before_down, live_down)
        pre_up = store_slot(pre_up, index_up, before_up, live_up)
        last_down = store_slot(last_down, index_down, next_down, live_down)
        last_up = store_slot(last_up, index_up, next_up, live_up)
        return (next_down, next_up, kept_down, kept_up, pre_down, pre_up, last_down, last_up)

    def forward_step(step_index, state):
        moved_down = shifted(state[0], "section", 1)
        moved_up = shifted(state[1], "section", -1)
        return forward_tick(step_index, (moved_down, moved_up) + state[2:])

    state = forward_tick(
        0,
        (
            blank_rows,
            blank_rows,
            blank_acts,
            blank_acts,
            blank_units,
            blank_units,
            blank_acts,
            blank_acts,
        ),
    )
    state = lax.fori_loop(1, tick_count, forward_step, state)
    kept_down, kept_up, pre_down, pre_up, last_down, last_up = state[2:]

    def backward_tick(step_index, state):
        from_right, from_left, seeds_down, seeds_up, dpre_down, dpre_up = state
        index_down, live_down = slot_of(step_index, final_section - position)
        index_up, live_up = slot_of(step_index, position)
        start_down = (seed_scale * read_slot(last_down, index_down).astype(jnp.float32)).astype(
            jnp.bfloat16
        )
        start_up = (seed_scale * read_slot(last_up, index_up).astype(jnp.float32)).astype(
            jnp.bfloat16
        )
        grad_down = jnp.where(position == final_section, start_down, from_right)
        grad_up = jnp.where(position == 0, start_up, from_left)
        back_down, dbefore_down = backward_section(
            read_slot(kept_down, index_down),
            read_slot(pre_down, index_down),
            in_down,
            out_down,
            grad_down,
        )
        back_up, dbefore_up = backward_section(
            read_slot(kept_up, index_up), read_slot(pre_up, index_up), in_up, out_up, grad_up
        )
        seeds_down = store_slot(seeds_down, index_down, grad_down, live_down)
        seeds_up = store_slot(seeds_up, index_up, grad_up, live_up)
        dpre_down = store_slot(dpre_down, index_down, dbefore_down, live_down)
        dpre_up = store_slot(dpre_up, index_up, dbefore_up, live_up)
        return (back_down, back_up, seeds_down, seeds_up, dpre_down, dpre_up)

    def backward_step(step_index, state):
        moved_down = shifted(state[0], "section", -1)
        moved_up = shifted(state[1], "section", 1)
        return backward_tick(step_index, (moved_down, moved_up) + state[2:])

    state = backward_tick(
        0, (blank_rows, blank_rows, blank_acts, blank_acts, blank_grads, blank_grads)
    )
    state = lax.fori_loop(1, tick_count, backward_step, state)
    seeds_down, seeds_up, dpre_down, dpre_up = state[2:]
    gin_down, gout_down = weight_terms(kept_down, pre_down, seeds_down, dpre_down)
    gin_up, gout_up = weight_terms(kept_up, pre_up, seeds_up, dpre_up)
    flat_up = jnp.stack([gin_up.reshape(section_count, -1), gout_up.reshape(section_count, -1)])
    outbound = lax.all_to_all(
        flat_up.astype(jnp.bfloat16), "section", split_axis=1, concat_axis=1, tiled=True
    ).astype(flat_up.dtype)
    returned = lax.all_to_all(
        jnp.flip(outbound, 1).astype(jnp.bfloat16),
        "section",
        split_axis=1,
        concat_axis=1,
        tiled=True,
    ).astype(jnp.float32)
    paired_in = gin_down + returned[0].reshape(gin_down.shape)
    paired_out = gout_down + returned[1].reshape(gout_down.shape)
    summed_in, summed_out = (
        lax.psum_scatter(
            paired_in.astype(jnp.bfloat16), "dp", scatter_dimension=0, tiled=True
        ).astype(jnp.float32),
        lax.psum_scatter(
            paired_out.astype(jnp.bfloat16), "dp", scatter_dimension=0, tiled=True
        ).astype(jnp.float32),
    )
    return (summed_in[None], summed_out[None])


def solution(mesh):
    in_specs = (
        P(None, None, "dp", None),
        P(None, "section", None, None),
        P(None, "section", None, None),
    )
    out_specs = (P("section", "dp", None), P("section", "dp", None))
    return jax.shard_map(
        per_device, mesh=mesh, in_specs=in_specs, out_specs=out_specs, check_vma=False
    )
```

profile of v0, /device:TPU:0, one launch (start us, length us, event | category | flops | bytes accessed | tf_op | source)
XLA Modules:
  0.0 595.1 jit_solution(9337617492887303649)
XLA Ops:
  8.3 2.2 slice_bitcast_fusion
  13.8 2.4 bitcast_dynamic-update-slice_fusion.10
  16.8 2.3 bitcast_dynamic-update-slice_fusion.14
  21.7 2.3 bitcast_dynamic-update-slice_fusion.15
  24.0 174.5 %while.52 = (s32[]{:T(128)}, bf16[16,512]{1,0:T(8,128)(2,1)}, bf16[16,512]{1,0:T(8,128)(2,1)}, bf16[4,16,512]{2,1,0:T(8,128)(2,1)S(1)}, bf16[4,16,512]{2,1,0:T(8...) while((s32[]{:T(128)}, bf16[16,512]{1,0:T(8,128)(2,1)}, ...), condition=%wide.region_5.6_spmd, body=%wide.region_2.5_spmd.sunk | while | flops 101154856 | bytes 15238702 | solution.py:113
  25.3 3.6 collective-permute-start
  34.9 2.5 bitcast_dynamic-update-slice_fusion.32
  41.6 5.1 collective-permute-start
  52.7 2.5 bitcast_dynamic-update-slice_fusion.32
  59.4 4.3 collective-permute-start
  69.7 2.5 bitcast_dynamic-update-slice_fusion.32
  76.4 4.3 collective-permute-start
  86.7 2.5 bitcast_dynamic-update-slice_fusion.32
  93.4 4.3 collective-permute-start
  103.7 2.5 bitcast_dynamic-update-slice_fusion.32
  110.4 5.1 collective-permute-start
  121.5 2.5 bitcast_dynamic-update-slice_fusion.32
  128.2 5.2 collective-permute-start
  139.4 2.5 bitcast_dynamic-update-slice_fusion.32
  146.1 5.2 collective-permute-start
  157.3 2.5 bitcast_dynamic-update-slice_fusion.32
  164.0 5.2 collective-permute-start
  175.2 2.5 bitcast_dynamic-update-slice_fusion.32
  181.9 5.2 collective-permute-start
  193.1 2.5 bitcast_dynamic-update-slice_fusion.32
  199.4 2.7 bitcast_dynamic-update-slice_fusion.12
  202.1 2.2 fusion.86
  205.1 2.0 bitcast_dynamic-update-slice_fusion.13
  212.1 156.8 %while.53 = (s32[]{:T(128)}, bf16[16,512]{1,0:T(8,128)(2,1)}, bf16[16,512]{1,0:T(8,128)(2,1)S(1)}, bf16[4,16,512]{2,1,0:T(8,128)(2,1)S(1)}, bf16[4,16,512]{2,1,0...) while((s32[]{:T(128)}, bf16[16,512]{1,0:T(8,128)(2,1)}, ...), condition=%wide.region_16.17_spmd, body=%wide.region_11.16_spmd.sunk | while | flops 101482536 | bytes 20874956 | solution.py:152
  212.1 4.0 collective-permute-start.3
  227.0 5.2 collective-permute-start.3
  243.0 5.2 collective-permute-start.3
  251.4 2.0 bitcast_dynamic-update-slice_fusion.37
  259.1 4.3 collective-permute-start.3
  266.6 2.0 bitcast_dynamic-update-slice_fusion.37
  274.2 4.3 collective-permute-start.3
  281.7 2.0 bitcast_dynamic-update-slice_fusion.37
  289.4 4.3 collective-permute-start.3
  296.9 2.0 bitcast_dynamic-update-slice_fusion.37
  304.6 5.2 collective-permute-start.3
  313.0 2.0 bitcast_dynamic-update-slice_fusion.37
  320.7 5.2 collective-permute-start.3
  329.1 2.0 bitcast_dynamic-update-slice_fusion.37
  332.6 2.1 bitcast_dynamic-update-slice_fusion.35
  336.8 5.2 collective-permute-start.3
  348.6 2.1 bitcast_dynamic-update-slice_fusion.35
  352.9 5.1 collective-permute-start.3
  364.7 2.0 bitcast_dynamic-update-slice_fusion.35
  368.9 2.8 fusion.52
  371.7 4.3 stack_reshape.10
  376.0 2.8 fusion.53
  378.8 6.0 %stack_reshape.11 = bf16[1,8,98304]{2,0,1:T(2,128)(2,1)} reshape(bf16[1536,512]{1,0:T(8,128)(2,1)} %fusion.53) | data formatting | bytes 3145728 | tf_op jit(solution)/shard_map/stack;reshape | solution.py:156
  384.8 8.3 %pad_maximum_fusion = bf16[2,8,98304]{2,0,1:T(2,128)(2,1)S(1)} fusion(bf16[1,8,98304]{2,0,1:T(2,128)(2,1)} %stack_reshape.11, bf16[1,8,98304]{2,0,1:T(2,128)(2,1)S(1)} %stack_reshape.10), kind=kLoop, calls=%fused_computation.113 | loop fusion | flops 6291456 | bytes 6291456 | tf_op jit(solution)/shard_map/stack | solution.py:156
  393.1 48.4 %all_to_all.10 = bf16[2,8,98304]{2,0,1:T(2,128)(2,1)S(1)} all-to-all(bf16[2,8,98304]{2,0,1:T(2,128)(2,1)S(1)} %pad_maximum_fusion), channel_id=1, replica_groups=mesh['section'=8,'dp'=4] {'section'}, dimensions={1} | all-to-all | bytes 6291456 | tf_op jit(solution)/shard_map/all_to_all | solution.py:157
  441.4 4.1 rev.6
  445.5 41.4 %all_to_all.11 = bf16[2,8,98304]{2,0,1:T(2,128)(2,1)S(1)} all-to-all(bf16[2,8,98304]{2,0,1:T(2,128)(2,1)} %rev.6), channel_id=1, replica_groups=mesh['section'=8,'dp'=4] {'section'}, dimensions={1} | all-to-all | bytes 6291456 | tf_op jit(solution)/shard_map/all_to_all | solution.py:160
  486.9 2.2 convert_element_type.341
  489.1 17.9 %slice_reduce_fusion = (f32[8,98304]{1,0:T(8,128)}, f32[8,98304]{1,0:T(8,128)S(1)}) fusion(f32[2,8,98304]{2,0,1:T(2,128)S(1)} %convert_element_type.341), kind=kLoop, calls=%fused_computation.111 | loop fusion | bytes 12582912 | tf_op jit(solution)/shard_map/slice | solution.py:168
  507.0 4.1 reshape_squeeze.7
  511.1 3.7 fusion.50
  515.8 2.2 reshape_squeeze.6
  518.0 3.8 fusion.51
  521.9 27.9 %reduce-scatter.5.cloned.1.call-done = bf16[384,512]{1,0:T(8,128)(2,1)} async-done(((bf16[1536,512]{1,0:T(8,128)(2,1)}), bf16[384,512]{1,0:T(8,128)(2,1)}) %reduce-scatter.5.cloned.1.call-update) | async-done | bytes 393232 | tf_op jit(solution)/shard_map/reduce_scatter | solution.py:173
  551.7 34.6 %reduce-scatter.3.cloned.1.call-done = bf16[128,1536]{1,0:T(8,128)(2,1)} async-done(((bf16[512,1536]{1,0:T(8,128)(2,1)}), bf16[128,1536]{1,0:T(8,128)(2,1)}) %reduce-scatter.3.cloned.1.call-update) | async-done | bytes 393232 | tf_op jit(solution)/shard_map/reduce_scatter | solution.py:170
  (548 shorter events, 209.3 us)
Async XLA Ops:
  7.2 542.6 %reduce-scatter.5.cloned.1.call-start = ((), (), s32[]{:S(2)}) async-start(), calls=%async_computation.5 | async-start | bytes 1966080 | tf_op jit(solution)/shard_map/reduce_scatter | solution.py:173
  24.0 6.2 %copy-start.8 = (bf16[4,16,512]{2,1,0:T(8,128)(2,1)}, bf16[4,16,512]{2,1,0:T(8,128)(2,1)S(1)}, u32[]{:S(2)}) copy-start(bf16[4,16,512]{2,1,0:T(8,128)(2,1)S(1)} %get-tuple-element.1186) | copy-start | bytes 196612 | tf_op jit(solution)/shard_map/while
  24.0 8.5 %collective-permute-start.1 = (bf16[16,512]{1,0:T(8,128)(2,1)}, bf16[16,512]{1,0:T(8,128)(2,1)}, u32[]{:S(2)}, u32[]{:S(2)}) collective-permute-start(bf16[16,512]{1,0:T(8,128)(2,1)} %get-tuple-element.1185), channel_id=1, source_target_pairs={{4,0},{8,4},{12,8},{16,12},{20,16},{24,20},{28,24},{5,1},{9,5},{13... | collective-permute-start | bytes 49160 | tf_op jit(solution)/shard_map/while/body/eval_jaxpr/ppermute | solution.py:10
  25.3 8.1 %collective-permute-start = (bf16[16,512]{1,0:T(8,128)(2,1)}, bf16[16,512]{1,0:T(8,128)(2,1)}, u32[]{:S(2)}, u32[]{:S(2)}) collective-permute-start(bf16[16,512]{1,0:T(8,128)(2,1)} %get-tuple-element.1184), channel_id=1, source_target_pairs={{0,4},{4,8},{8,12},{12,16},{16,20},{20,24},{24,28},{1,5},{5,9},{9,... | collective-permute-start | bytes 49160 | tf_op jit(solution)/shard_map/while/body/eval_jaxpr/ppermute | solution.py:10
  40.3 7.7 %copy-start.8 = (bf16[4,16,512]{2,1,0:T(8,128)(2,1)}, bf16[4,16,512]{2,1,0:T(8,128)(2,1)S(1)}, u32[]{:S(2)}) copy-start(bf16[4,16,512]{2,1,0:T(8,128)(2,1)S(1)} %get-tuple-element.1186) | copy-start | bytes 196612 | tf_op jit(solution)/shard_map/while
  40.3 10.0 %collective-permute-start.1 = (bf16[16,512]{1,0:T(8,128)(2,1)}, bf16[16,512]{1,0:T(8,128)(2,1)}, u32[]{:S(2)}, u32[]{:S(2)}) collective-permute-start(bf16[16,512]{1,0:T(8,128)(2,1)} %get-tuple-element.1185), channel_id=1, source_target_pairs={{4,0},{8,4},{12,8},{16,12},{20,16},{24,20},{28,24},{5,1},{9,5},{13... | collective-permute-start | bytes 49160 | tf_op jit(solution)/shard_map/while/body/eval_jaxpr/ppermute | solution.py:10
  41.6 9.6 %collective-permute-start = (bf16[16,512]{1,0:T(8,128)(2,1)}, bf16[16,512]{1,0:T(8,128)(2,1)}, u32[]{:S(2)}, u32[]{:S(2)}) collective-permute-start(bf16[16,512]{1,0:T(8,128)(2,1)} %get-tuple-element.1184), channel_id=1, source_target_pairs={{0,4},{4,8},{8,12},{12,16},{16,20},{20,24},{24,28},{1,5},{5,9},{9,... | collective-permute-start | bytes 49160 | tf_op jit(solution)/shard_map/while/body/eval_jaxpr/ppermute | solution.py:10
  58.1 6.9 %copy-start.8 = (bf16[4,16,512]{2,1,0:T(8,128)(2,1)}, bf16[4,16,512]{2,1,0:T(8,128)(2,1)S(1)}, u32[]{:S(2)}) copy-start(bf16[4,16,512]{2,1,0:T(8,128)(2,1)S(1)} %get-tuple-element.1186) | copy-start | bytes 196612 | tf_op jit(solution)/shard_map/while
  58.1 9.2 %collective-permute-start.1 = (bf16[16,512]{1,0:T(8,128)(2,1)}, bf16[16,512]{1,0:T(8,128)(2,1)}, u32[]{:S(2)}, u32[]{:S(2)}) collective-permute-start(bf16[16,512]{1,0:T(8,128)(2,1)} %get-tuple-element.1185), channel_id=1, source_target_pairs={{4,0},{8,4},{12,8},{16,12},{20,16},{24,20},{28,24},{5,1},{9,5},{13... | collective-permute-start | bytes 49160 | tf_op jit(solution)/shard_map/while/body/eval_jaxpr/ppermute | solution.py:10
  59.4 8.8 %collective-permute-start = (bf16[16,512]{1,0:T(8,128)(2,1)}, bf16[16,512]{1,0:T(8,128)(2,1)}, u32[]{:S(2)}, u32[]{:S(2)}) collective-permute-start(bf16[16,512]{1,0:T(8,128)(2,1)} %get-tuple-element.1184), channel_id=1, source_target_pairs={{0,4},{4,8},{8,12},{12,16},{16,20},{20,24},{24,28},{1,5},{5,9},{9,... | collective-permute-start | bytes 49160 | tf_op jit(solution)/shard_map/while/body/eval_jaxpr/ppermute | solution.py:10
  75.2 6.9 %copy-start.8 = (bf16[4,16,512]{2,1,0:T(8,128)(2,1)}, bf16[4,16,512]{2,1,0:T(8,128)(2,1)S(1)}, u32[]{:S(2)}) copy-start(bf16[4,16,512]{2,1,0:T(8,128)(2,1)S(1)} %get-tuple-element.1186) | copy-start | bytes 196612 | tf_op jit(solution)/shard_map/while
  75.2 9.2 %collective-permute-start.1 = (bf16[16,512]{1,0:T(8,128)(2,1)}, bf16[16,512]{1,0:T(8,128)(2,1)}, u32[]{:S(2)}, u32[]{:S(2)}) collective-permute-start(bf16[16,512]{1,0:T(8,128)(2,1)} %get-tuple-element.1185), channel_id=1, source_target_pairs={{4,0},{8,4},{12,8},{16,12},{20,16},{24,20},{28,24},{5,1},{9,5},{13... | collective-permute-start | bytes 49160 | tf_op jit(solution)/shard_map/while/body/eval_jaxpr/ppermute | solution.py:10
  76.4 8.8 %collective-permute-start = (bf16[16,512]{1,0:T(8,128)(2,1)}, bf16[16,512]{1,0:T(8,128)(2,1)}, u32[]{:S(2)}, u32[]{:S(2)}) collective-permute-start(bf16[16,512]{1,0:T(8,128)(2,1)} %get-tuple-element.1184), channel_id=1, source_target_pairs={{0,4},{4,8},{8,12},{12,16},{16,20},{20,24},{24,28},{1,5},{5,9},{9,... | collective-permute-start | bytes 49160 | tf_op jit(solution)/shard_map/while/body/eval_jaxpr/ppermute | solution.py:10
  92.1 6.9 %copy-start.8 = (bf16[4,16,512]{2,1,0:T(8,128)(2,1)}, bf16[4,16,512]{2,1,0:T(8,128)(2,1)S(1)}, u32[]{:S(2)}) copy-start(bf16[4,16,512]{2,1,0:T(8,128)(2,1)S(1)} %get-tuple-element.1186) | copy-start | bytes 196612 | tf_op jit(solution)/shard_map/while
  92.1 9.2 %collective-permute-start.1 = (bf16[16,512]{1,0:T(8,128)(2,1)}, bf16[16,512]{1,0:T(8,128)(2,1)}, u32[]{:S(2)}, u32[]{:S(2)}) collective-permute-start(bf16[16,512]{1,0:T(8,128)(2,1)} %get-tuple-element.1185), channel_id=1, source_target_pairs={{4,0},{8,4},{12,8},{16,12},{20,16},{24,20},{28,24},{5,1},{9,5},{13... | collective-permute-start | bytes 49160 | tf_op jit(solution)/shard_map/while/body/eval_jaxpr/ppermute | solution.py:10
  93.4 8.8 %collective-permute-start = (bf16[16,512]{1,0:T(8,128)(2,1)}, bf16[16,512]{1,0:T(8,128)(2,1)}, u32[]{:S(2)}, u32[]{:S(2)}) collective-permute-start(bf16[16,512]{1,0:T(8,128)(2,1)} %get-tuple-element.1184), channel_id=1, source_target_pairs={{0,4},{4,8},{8,12},{12,16},{16,20},{20,24},{24,28},{1,5},{5,9},{9,... | collective-permute-start | bytes 49160 | tf_op jit(solution)/shard_map/while/body/eval_jaxpr/ppermute | solution.py:10
  109.1 7.7 %copy-start.8 = (bf16[4,16,512]{2,1,0:T(8,128)(2,1)}, bf16[4,16,512]{2,1,0:T(8,128)(2,1)S(1)}, u32[]{:S(2)}) copy-start(bf16[4,16,512]{2,1,0:T(8,128)(2,1)S(1)} %get-tuple-element.1186) | copy-start | bytes 196612 | tf_op jit(solution)/shard_map/while
  109.1 10.0 %collective-permute-start.1 = (bf16[16,512]{1,0:T(8,128)(2,1)}, bf16[16,512]{1,0:T(8,128)(2,1)}, u32[]{:S(2)}, u32[]{:S(2)}) collective-permute-start(bf16[16,512]{1,0:T(8,128)(2,1)} %get-tuple-element.1185), channel_id=1, source_target_pairs={{4,0},{8,4},{12,8},{16,12},{20,16},{24,20},{28,24},{5,1},{9,5},{13... | collective-permute-start | bytes 49160 | tf_op jit(solution)/shard_map/while/body/eval_jaxpr/ppermute | solution.py:10
  110.4 9.6 %collective-permute-start = (bf16[16,512]{1,0:T(8,128)(2,1)}, bf16[16,512]{1,0:T(8,128)(2,1)}, u32[]{:S(2)}, u32[]{:S(2)}) collective-permute-start(bf16[16,512]{1,0:T(8,128)(2,1)} %get-tuple-element.1184), channel_id=1, source_target_pairs={{0,4},{4,8},{8,12},{12,16},{16,20},{20,24},{24,28},{1,5},{5,9},{9,... | collective-permute-start | bytes 49160 | tf_op jit(solution)/shard_map/while/body/eval_jaxpr/ppermute | solution.py:10
  126.9 7.8 %copy-start.8 = (bf16[4,16,512]{2,1,0:T(8,128)(2,1)}, bf16[4,16,512]{2,1,0:T(8,128)(2,1)S(1)}, u32[]{:S(2)}) copy-start(bf16[4,16,512]{2,1,0:T(8,128)(2,1)S(1)} %get-tuple-element.1186) | copy-start | bytes 196612 | tf_op jit(solution)/shard_map/while
  126.9 10.1 %collective-permute-start.1 = (bf16[16,512]{1,0:T(8,128)(2,1)}, bf16[16,512]{1,0:T(8,128)(2,1)}, u32[]{:S(2)}, u32[]{:S(2)}) collective-permute-start(bf16[16,512]{1,0:T(8,128)(2,1)} %get-tuple-element.1185), channel_id=1, source_target_pairs={{4,0},{8,4},{12,8},{16,12},{20,16},{24,20},{28,24},{5,1},{9,5},{13... | collective-permute-start | bytes 49160 | tf_op jit(solution)/shard_map/while/body/eval_jaxpr/ppermute | solution.py:10
  128.2 9.7 %collective-permute-start = (bf16[16,512]{1,0:T(8,128)(2,1)}, bf16[16,512]{1,0:T(8,128)(2,1)}, u32[]{:S(2)}, u32[]{:S(2)}) collective-permute-start(bf16[16,512]{1,0:T(8,128)(2,1)} %get-tuple-element.1184), channel_id=1, source_target_pairs={{0,4},{4,8},{8,12},{12,16},{16,20},{20,24},{24,28},{1,5},{5,9},{9,... | collective-permute-start | bytes 49160 | tf_op jit(solution)/shard_map/while/body/eval_jaxpr/ppermute | solution.py:10
  144.8 7.8 %copy-start.8 = (bf16[4,16,512]{2,1,0:T(8,128)(2,1)}, bf16[4,16,512]{2,1,0:T(8,128)(2,1)S(1)}, u32[]{:S(2)}) copy-start(bf16[4,16,512]{2,1,0:T(8,128)(2,1)S(1)} %get-tuple-element.1186) | copy-start | bytes 196612 | tf_op jit(solution)/shard_map/while
  144.8 10.1 %collective-permute-start.1 = (bf16[16,512]{1,0:T(8,128)(2,1)}, bf16[16,512]{1,0:T(8,128)(2,1)}, u32[]{:S(2)}, u32[]{:S(2)}) collective-permute-start(bf16[16,512]{1,0:T(8,128)(2,1)} %get-tuple-element.1185), channel_id=1, source_target_pairs={{4,0},{8,4},{12,8},{16,12},{20,16},{24,20},{28,24},{5,1},{9,5},{13... | collective-permute-start | bytes 49160 | tf_op jit(solution)/shard_map/while/body/eval_jaxpr/ppermute | solution.py:10
  146.1 9.7 %collective-permute-start = (bf16[16,512]{1,0:T(8,128)(2,1)}, bf16[16,512]{1,0:T(8,128)(2,1)}, u32[]{:S(2)}, u32[]{:S(2)}) collective-permute-start(bf16[16,512]{1,0:T(8,128)(2,1)} %get-tuple-element.1184), channel_id=1, source_target_pairs={{0,4},{4,8},{8,12},{12,16},{16,20},{20,24},{24,28},{1,5},{5,9},{9,... | collective-permute-start | bytes 49160 | tf_op jit(solution)/shard_map/while/body/eval_jaxpr/ppermute | solution.py:10
  162.7 7.8 %copy-start.8 = (bf16[4,16,512]{2,1,0:T(8,128)(2,1)}, bf16[4,16,512]{2,1,0:T(8,128)(2,1)S(1)}, u32[]{:S(2)}) copy-start(bf16[4,16,512]{2,1,0:T(8,128)(2,1)S(1)} %get-tuple-element.1186) | copy-start | bytes 196612 | tf_op jit(solution)/shard_map/while
  162.7 10.1 %collective-permute-start.1 = (bf16[16,512]{1,0:T(8,128)(2,1)}, bf16[16,512]{1,0:T(8,128)(2,1)}, u32[]{:S(2)}, u32[]{:S(2)}) collective-permute-start(bf16[16,512]{1,0:T(8,128)(2,1)} %get-tuple-element.1185), channel_id=1, source_target_pairs={{4,0},{8,4},{12,8},{16,12},{20,16},{24,20},{28,24},{5,1},{9,5},{13... | collective-permute-start | bytes 49160 | tf_op jit(solution)/shard_map/while/body/eval_jaxpr/ppermute | solution.py:10
  164.0 9.7 %collective-permute-start = (bf16[16,512]{1,0:T(8,128)(2,1)}, bf16[16,512]{1,0:T(8,128)(2,1)}, u32[]{:S(2)}, u32[]{:S(2)}) collective-permute-start(bf16[16,512]{1,0:T(8,128)(2,1)} %get-tuple-element.1184), channel_id=1, source_target_pairs={{0,4},{4,8},{8,12},{12,16},{16,20},{20,24},{24,28},{1,5},{5,9},{9,... | collective-permute-start | bytes 49160 | tf_op jit(solution)/shard_map/while/body/eval_jaxpr/ppermute | solution.py:10
  180.6 7.8 %copy-start.8 = (bf16[4,16,512]{2,1,0:T(8,128)(2,1)}, bf16[4,16,512]{2,1,0:T(8,128)(2,1)S(1)}, u32[]{:S(2)}) copy-start(bf16[4,16,512]{2,1,0:T(8,128)(2,1)S(1)} %get-tuple-element.1186) | copy-start | bytes 196612 | tf_op jit(solution)/shard_map/while
  180.6 10.1 %collective-permute-start.1 = (bf16[16,512]{1,0:T(8,128)(2,1)}, bf16[16,512]{1,0:T(8,128)(2,1)}, u32[]{:S(2)}, u32[]{:S(2)}) collective-permute-start(bf16[16,512]{1,0:T(8,128)(2,1)} %get-tuple-element.1185), channel_id=1, source_target_pairs={{4,0},{8,4},{12,8},{16,12},{20,16},{24,20},{28,24},{5,1},{9,5},{13... | collective-permute-start | bytes 49160 | tf_op jit(solution)/shard_map/while/body/eval_jaxpr/ppermute | solution.py:10
  181.9 9.7 %collective-permute-start = (bf16[16,512]{1,0:T(8,128)(2,1)}, bf16[16,512]{1,0:T(8,128)(2,1)}, u32[]{:S(2)}, u32[]{:S(2)}) collective-permute-start(bf16[16,512]{1,0:T(8,128)(2,1)} %get-tuple-element.1184), channel_id=1, source_target_pairs={{0,4},{4,8},{8,12},{12,16},{16,20},{20,24},{24,28},{1,5},{5,9},{9,... | collective-permute-start | bytes 49160 | tf_op jit(solution)/shard_map/while/body/eval_jaxpr/ppermute | solution.py:10
  199.4 5.7 copy-start.14
  202.1 5.1 copy-start.4
  212.1 5.5 copy-start.10
  212.1 6.3 %collective-permute-start.3 = (bf16[16,512]{1,0:T(8,128)(2,1)S(1)}, bf16[16,512]{1,0:T(8,128)(2,1)S(1)}, u32[]{:S(2)}, u32[]{:S(2)}) collective-permute-start(bf16[16,512]{1,0:T(8,128)(2,1)S(1)} %get-tuple-element.1254), channel_id=1, source_target_pairs={{0,4},{4,8},{8,12},{12,16},{16,20},{20,24},{24,28},{1,5},{5,9},{9,... | collective-permute-start | bytes 49160 | tf_op jit(solution)/shard_map/while/body/eval_jaxpr/ppermute | solution.py:10
  216.1 5.9 collective-permute-start.2
  227.0 6.6 %copy-start.10 = (bf16[4,16,512]{2,1,0:T(8,128)(2,1)}, bf16[4,16,512]{2,1,0:T(8,128)(2,1)S(1)}, u32[]{:S(2)}) copy-start(bf16[4,16,512]{2,1,0:T(8,128)(2,1)S(1)} %get-tuple-element.1287) | copy-start | bytes 196612 | tf_op jit(solution)/shard_map/while
  227.0 7.5 %collective-permute-start.3 = (bf16[16,512]{1,0:T(8,128)(2,1)S(1)}, bf16[16,512]{1,0:T(8,128)(2,1)S(1)}, u32[]{:S(2)}, u32[]{:S(2)}) collective-permute-start(bf16[16,512]{1,0:T(8,128)(2,1)S(1)} %get-tuple-element.1254), channel_id=1, source_target_pairs={{0,4},{4,8},{8,12},{12,16},{16,20},{20,24},{24,28},{1,5},{5,9},{9,... | collective-permute-start | bytes 49160 | tf_op jit(solution)/shard_map/while/body/eval_jaxpr/ppermute | solution.py:10
  232.1 5.9 collective-permute-start.2
  243.0 6.6 %copy-start.10 = (bf16[4,16,512]{2,1,0:T(8,128)(2,1)}, bf16[4,16,512]{2,1,0:T(8,128)(2,1)S(1)}, u32[]{:S(2)}) copy-start(bf16[4,16,512]{2,1,0:T(8,128)(2,1)S(1)} %get-tuple-element.1287) | copy-start | bytes 196612 | tf_op jit(solution)/shard_map/while
  243.0 7.5 %collective-permute-start.3 = (bf16[16,512]{1,0:T(8,128)(2,1)S(1)}, bf16[16,512]{1,0:T(8,128)(2,1)S(1)}, u32[]{:S(2)}, u32[]{:S(2)}) collective-permute-start(bf16[16,512]{1,0:T(8,128)(2,1)S(1)} %get-tuple-element.1254), channel_id=1, source_target_pairs={{0,4},{4,8},{8,12},{12,16},{16,20},{20,24},{24,28},{1,5},{5,9},{9,... | collective-permute-start | bytes 49160 | tf_op jit(solution)/shard_map/while/body/eval_jaxpr/ppermute | solution.py:10
  248.2 5.9 collective-permute-start.2
  259.1 5.7 copy-start.10
  259.1 6.6 %collective-permute-start.3 = (bf16[16,512]{1,0:T(8,128)(2,1)S(1)}, bf16[16,512]{1,0:T(8,128)(2,1)S(1)}, u32[]{:S(2)}, u32[]{:S(2)}) collective-permute-start(bf16[16,512]{1,0:T(8,128)(2,1)S(1)} %get-tuple-element.1254), channel_id=1, source_target_pairs={{0,4},{4,8},{8,12},{12,16},{16,20},{20,24},{24,28},{1,5},{5,9},{9,... | collective-permute-start | bytes 49160 | tf_op jit(solution)/shard_map/while/body/eval_jaxpr/ppermute | solution.py:10
  263.3 5.9 collective-permute-start.2
  274.2 5.7 copy-start.10
  274.2 6.6 %collective-permute-start.3 = (bf16[16,512]{1,0:T(8,128)(2,1)S(1)}, bf16[16,512]{1,0:T(8,128)(2,1)S(1)}, u32[]{:S(2)}, u32[]{:S(2)}) collective-permute-start(bf16[16,512]{1,0:T(8,128)(2,1)S(1)} %get-tuple-element.1254), channel_id=1, source_target_pairs={{0,4},{4,8},{8,12},{12,16},{16,20},{20,24},{24,28},{1,5},{5,9},{9,... | collective-permute-start | bytes 49160 | tf_op jit(solution)/shard_map/while/body/eval_jaxpr/ppermute | solution.py:10
  278.5 5.9 collective-permute-start.2
  289.4 5.8 copy-start.10
  289.4 6.7 %collective-permute-start.3 = (bf16[16,512]{1,0:T(8,128)(2,1)S(1)}, bf16[16,512]{1,0:T(8,128)(2,1)S(1)}, u32[]{:S(2)}, u32[]{:S(2)}) collective-permute-start(bf16[16,512]{1,0:T(8,128)(2,1)S(1)} %get-tuple-element.1254), channel_id=1, source_target_pairs={{0,4},{4,8},{8,12},{12,16},{16,20},{20,24},{24,28},{1,5},{5,9},{9,... | collective-permute-start | bytes 49160 | tf_op jit(solution)/shard_map/while/body/eval_jaxpr/ppermute | solution.py:10
  293.7 5.9 collective-permute-start.2
  304.6 6.6 %copy-start.10 = (bf16[4,16,512]{2,1,0:T(8,128)(2,1)}, bf16[4,16,512]{2,1,0:T(8,128)(2,1)S(1)}, u32[]{:S(2)}) copy-start(bf16[4,16,512]{2,1,0:T(8,128)(2,1)S(1)} %get-tuple-element.1287) | copy-start | bytes 196612 | tf_op jit(solution)/shard_map/while
  304.6 7.5 %collective-permute-start.3 = (bf16[16,512]{1,0:T(8,128)(2,1)S(1)}, bf16[16,512]{1,0:T(8,128)(2,1)S(1)}, u32[]{:S(2)}, u32[]{:S(2)}) collective-permute-start(bf16[16,512]{1,0:T(8,128)(2,1)S(1)} %get-tuple-element.1254), channel_id=1, source_target_pairs={{0,4},{4,8},{8,12},{12,16},{16,20},{20,24},{24,28},{1,5},{5,9},{9,... | collective-permute-start | bytes 49160 | tf_op jit(solution)/shard_map/while/body/eval_jaxpr/ppermute | solution.py:10
  309.8 5.9 collective-permute-start.2
  320.7 6.7 %copy-start.10 = (bf16[4,16,512]{2,1,0:T(8,128)(2,1)}, bf16[4,16,512]{2,1,0:T(8,128)(2,1)S(1)}, u32[]{:S(2)}) copy-start(bf16[4,16,512]{2,1,0:T(8,128)(2,1)S(1)} %get-tuple-element.1287) | copy-start | bytes 196612 | tf_op jit(solution)/shard_map/while
  320.7 7.6 %collective-permute-start.3 = (bf16[16,512]{1,0:T(8,128)(2,1)S(1)}, bf16[16,512]{1,0:T(8,128)(2,1)S(1)}, u32[]{:S(2)}, u32[]{:S(2)}) collective-permute-start(bf16[16,512]{1,0:T(8,128)(2,1)S(1)} %get-tuple-element.1254), channel_id=1, source_target_pairs={{0,4},{4,8},{8,12},{12,16},{16,20},{20,24},{24,28},{1,5},{5,9},{9,... | collective-permute-start | bytes 49160 | tf_op jit(solution)/shard_map/while/body/eval_jaxpr/ppermute | solution.py:10
  325.9 5.9 collective-permute-start.2
  336.8 6.7 %copy-start.10 = (bf16[4,16,512]{2,1,0:T(8,128)(2,1)}, bf16[4,16,512]{2,1,0:T(8,128)(2,1)S(1)}, u32[]{:S(2)}) copy-start(bf16[4,16,512]{2,1,0:T(8,128)(2,1)S(1)} %get-tuple-element.1287) | copy-start | bytes 196612 | tf_op jit(solution)/shard_map/while
  336.8 7.5 %collective-permute-start.3 = (bf16[16,512]{1,0:T(8,128)(2,1)S(1)}, bf16[16,512]{1,0:T(8,128)(2,1)S(1)}, u32[]{:S(2)}, u32[]{:S(2)}) collective-permute-start(bf16[16,512]{1,0:T(8,128)(2,1)S(1)} %get-tuple-element.1254), channel_id=1, source_target_pairs={{0,4},{4,8},{8,12},{12,16},{16,20},{20,24},{24,28},{1,5},{5,9},{9,... | collective-permute-start | bytes 49160 | tf_op jit(solution)/shard_map/while/body/eval_jaxpr/ppermute | solution.py:10
  342.0 5.9 collective-permute-start.2
  352.9 6.6 %copy-start.10 = (bf16[4,16,512]{2,1,0:T(8,128)(2,1)}, bf16[4,16,512]{2,1,0:T(8,128)(2,1)S(1)}, u32[]{:S(2)}) copy-start(bf16[4,16,512]{2,1,0:T(8,128)(2,1)S(1)} %get-tuple-element.1287) | copy-start | bytes 196612 | tf_op jit(solution)/shard_map/while
  352.9 7.5 %collective-permute-start.3 = (bf16[16,512]{1,0:T(8,128)(2,1)S(1)}, bf16[16,512]{1,0:T(8,128)(2,1)S(1)}, u32[]{:S(2)}, u32[]{:S(2)}) collective-permute-start(bf16[16,512]{1,0:T(8,128)(2,1)S(1)} %get-tuple-element.1254), channel_id=1, source_target_pairs={{0,4},{4,8},{8,12},{12,16},{16,20},{20,24},{24,28},{1,5},{5,9},{9,... | collective-permute-start | bytes 49160 | tf_op jit(solution)/shard_map/while/body/eval_jaxpr/ppermute | solution.py:10
  358.0 5.9 collective-permute-start.2
  514.9 71.4 %reduce-scatter.3.cloned.1.call-start = ((), (), s32[]{:S(2)}) async-start(), calls=%async_computation.4 | async-start | bytes 1966080 | tf_op jit(solution)/shard_map/reduce_scatter | solution.py:170
  (67 other events, 193.5 us)
Sparse Core Ops, SparseCore 0:
  515.0 34.6 reduce-scatter.4
  552.0 34.2 reduce-scatter.2
where the time goes:
time: 604 us; the launch traced here: 595 us
  matrix products  145 us (24%)
  starting transfers between devices  121 us (20%)
  local copies, waits for them, and re-layouts  92.9 us (15%)
  blocking collectives  89.8 us (15%)
  other arithmetic  67.9 us (11%)
  waiting for transfers between devices  62.6 us (10%)
  between operations  14.2 us (2%)
    ppermute x40, starting transfers between devices, shifted(): lax.ppermute(value, axis, [(source, source + steps) for source in range(f...  121 us
    all_to_all x1, blocking collectives, per_device(): lax.all_to_all(flat_up.astype(jnp.bfloat16), 'section', split_axis=1, con...  48.4 us
    dot_general x22, matrix products, backward_section(): jnp.einsum('md,rd->mr', incoming, weight_out, preferred_element_type=jnp....  45.6 us
    all_to_all x1, blocking collectives, per_device(): lax.all_to_all(jnp.flip(outbound, 1).astype(jnp.bfloat16), 'section', spl...  41.4 us
    dot_general x22, matrix products, forward_section(): before = jnp.dot(normed, weight_in, preferred_element_type=jnp.float32)  39.6 us
    dynamic_update_slice x44, other arithmetic, store_slot(): lax.dynamic_update_index_in_dim(buffer, jnp.where(valid, value, old_value...  38.5 us
    dynamic_slice x50, local copies, waits for them, and re-layouts, read_slot(): return lax.dynamic_index_in_dim(buffer, index, 0, keepdims=False)  37.6 us
    reduce_scatter x1, waiting for transfers between devices, per_device(): lax.psum_scatter(paired_in.astype(jnp.bfloat16), 'dp', scatter_dimension=...  34.6 us
  transfers between devices with their start and end apart: 42, of which 2 were waited for; matrix products, arithmetic and copies ran while one was open for 16% of the time, Pallas kernels for 0%

commit v1 on v0

v1 whole, which is shorter than its diff:
```python
import functools

import jax
import jax.numpy as jnp
from jax import lax
from jax.experimental import pallas as pl
from jax.experimental.pallas import tpu as pltpu
from jax.sharding import PartitionSpec as P

MESH = pl.DeviceIdType.MESH
F32, BF16 = jnp.float32, jnp.bfloat16
HOP_CHUNKS = 2
UNIT_CHUNKS = 3


def dot(a, b):
    return jnp.dot(a, b, preferred_element_type=F32)


def dot_nt(a, b):
    return lax.dot_general(a, b, (((1,), (1,)), ((), ())), preferred_element_type=F32)


def norm_factor(wide):
    return lax.rsqrt(jnp.mean(wide * wide, axis=-1, keepdims=True) + 1e-05)


def relay_kernel(
    S, DP, scale,
    feed, win, wout, oa, ob,
    wa, wb, h_all, g_all, h_out, g_out, pre_own, dsl_own, hid_own, dpre_own, u_own, r_own,
    n_t, h_t, dsl_all, up_a, up_b, got_a, got_b, full_t,
    load_sem, feed_sem, hop_send, hop_recv, all_send, all_recv, up_send, up_recv,
):
    s, d = lax.axis_index("section"), lax.axis_index("dp")
    M, D = h_all.shape[2], h_all.shape[3]
    R = wa.shape[2]
    T = DP * M
    ra, rb = D // DP, R // DP
    half = S // 2
    p0 = s // half
    p1 = 1 - p0
    k0 = s + p0 * (S - 1 - 2 * s)
    mirror = S - 1 - s
    cw, uw = D // HOP_CHUNKS, R // UNIT_CHUNKS

    def load(i, src, dst, p):
        return pltpu.make_async_copy(src.at[p, 0], dst.at[p], load_sem.at[i, p])

    feed_copy = pltpu.make_async_copy(feed.at[p0], h_all.at[p0, d], feed_sem)

    @pl.when(k0 == 0)
    def _():
        feed_copy.start()

    for p in (p0, p1):
        load(0, win, wa, p).start()
        load(1, wout, wb, p).start()

    barrier = pltpu.get_barrier_semaphore()
    for other in (lax.rem(s + 1, S), lax.rem(s + S - 1, S), mirror):
        pl.semaphore_signal(barrier, inc=1, device_id={"section": other}, device_id_type=MESH)
    for o in range(1, DP):
        pl.semaphore_signal(
            barrier, inc=1, device_id={"dp": lax.rem(d + o, DP)}, device_id_type=MESH
        )
    pl.semaphore_wait(barrier, 3 + DP - 1)

    def hop(kind, p, c):
        step = 1 - 2 * p
        peer = s + step if kind == 0 else s - step
        src, dst = (h_out, h_all) if kind == 0 else (g_out, g_all)
        cols = pl.ds(c * cw, cw)
        return pltpu.make_async_remote_copy(
            src_ref=src.at[p, :, cols],
            dst_ref=dst.at[p, d, :, cols],
            send_sem=hop_send.at[kind, p, c],
            recv_sem=hop_recv.at[kind, p, c],
            device_id={"section": peer},
            device_id_type=MESH,
        )

    def share(kind, p, o):
        buf = h_all if kind == 0 else g_all
        return pltpu.make_async_remote_copy(
            src_ref=buf.at[p, d],
            dst_ref=buf.at[p, d],
            send_sem=all_send.at[kind, p, o - 1],
            recv_sem=all_recv.at[kind, p, o - 1],
            device_id={"dp": lax.rem(d + o, DP)},
            device_id_type=MESH,
        )

    def take(kind, p, o):
        buf = h_all if kind == 0 else g_all
        source = lax.rem(d + DP - o, DP)
        return pltpu.make_async_remote_copy(
            src_ref=buf.at[p, source],
            dst_ref=buf.at[p, source],
            send_sem=all_send.at[kind, p, o - 1],
            recv_sem=all_recv.at[kind, p, o - 1],
            device_id={"dp": source},
            device_id_type=MESH,
        )

    def share_start(kind, p):
        for o in range(1, DP):
            share(kind, p, o).start()

    def take_wait(kind, p):
        for o in range(1, DP):
            take(kind, p, o).wait_recv()

    def up_copy(i):
        src, dst = ((up_b, got_b), (up_a, got_a))[min(i, 1)]
        if i:
            cols = pl.ds((i - 1) * uw, uw)
            src, dst = src.at[:, cols], dst.at[:, cols]
        return pltpu.make_async_remote_copy(
            src_ref=src,
            dst_ref=dst,
            send_sem=up_send.at[i],
            recv_sem=up_recv.at[i],
            device_id={"section": mirror},
            device_id_type=MESH,
        )

    def forward(p, sends):
        wide = h_all[p, d].astype(F32)
        factor = norm_factor(wide)
        scaled = wide * factor
        normed = scaled.astype(BF16)
        for c in range(UNIT_CHUNKS):
            cols = pl.ds(c * uw, uw)
            before = dot(normed, wa[p, :, cols])
            hid_own[:, cols] = (before * jax.nn.sigmoid(before)).astype(BF16)
            pre_own[p, :, cols] = before
        for c in range(HOP_CHUNKS):
            cols = pl.ds(c * cw, cw)
            old = h_all[p, d, :, cols].astype(F32)
            h_out[p, :, cols] = (old + dot(hid_own[...], wb[p, :, cols])).astype(BF16)

            @pl.when(sends)
            def _():
                hop(0, p, c).start()

        share_start(0, p)
        u_own[p] = scaled
        r_own[p] = jnp.broadcast_to(factor, (M, 128))
        for c in range(UNIT_CHUNKS):
            cols = pl.ds(c * uw, uw)
            before = pre_own[p, :, cols]
            sigma = jax.nn.sigmoid(before)
            dsl_own[p, :, cols] = sigma * (1.0 + before * (1.0 - sigma))

    def backward(p):
        incoming = g_all[p, d]
        total = jnp.zeros((M, 1), F32)
        for c in range(UNIT_CHUNKS):
            cols = pl.ds(c * uw, uw)
            d_hidden = dot_nt(incoming, wb[p, cols, :])
            d_before = (d_hidden * dsl_own[p, :, cols]).astype(BF16)
            dpre_own[:, cols] = d_before
            total += jnp.sum(
                d_before.astype(F32) * pre_own[p, :, cols], axis=-1, keepdims=True
            )
        mean = total * (1.0 / D)
        factor = r_own[p, :, 0:1]
        for c in range(HOP_CHUNKS):
            cols = pl.ds(c * cw, cw)
            d_normed = dot_nt(dpre_own[...], wa[p, cols, :])
            out = g_all[p, d, :, cols].astype(F32) + factor * (
                d_normed - u_own[p, :, cols] * mean
            )
            g_out[p, :, cols] = out.astype(BF16)
            hop(1, p, c).start()

    aligned = ra % 128 == 0 and rb % 128 == 0
    block = min(T, 256)

    def prepare(p):
        take_wait(0, p)

        def rows_step(b):
            per = block // M
            rows = pl.ds(pl.multiple_of(b * block, block), block)
            wide = h_all[p, pl.ds(b * per, per)].reshape(block, D).astype(F32)
            normed_wide = wide * norm_factor(wide)
            normed = normed_wide.astype(BF16)
            if aligned:
                mine = h_all[
                    p, pl.ds(b * per, per), :, pl.ds(pl.multiple_of(d * ra, 128), ra)
                ].reshape(block, ra).astype(F32) * norm_factor(wide)
                n_t[p, :, rows] = mine.T.astype(BF16)
            else:
                full_t[0:D, rows] = normed_wide.T.astype(BF16)
            for c in range(UNIT_CHUNKS):
                cols = pl.ds(c * uw, uw)
                before = dot(normed, wa[p, :, cols])
                sigma = jax.nn.sigmoid(before)
                hidden = before * sigma
                dsl_all[p, rows, cols] = sigma * (1.0 + before * (1.0 - sigma))
                if not aligned:
                    full_t[D + c * uw:D + (c + 1) * uw, rows] = hidden.T.astype(BF16)
            if aligned:
                before = dot(normed, wa[p, :, pl.ds(pl.multiple_of(d * rb, 128), rb)])
                hidden = before * jax.nn.sigmoid(before)
                h_t[p, :, rows] = hidden.T.astype(BF16)

        if T == block:
            rows_step(0)
        else:
            pl.loop(0, T // block)(rows_step)
        if not aligned:
            n_t[p] = full_t[pl.ds(pl.multiple_of(d * ra, 16), ra), :]
            h_t[p] = full_t[pl.ds(pl.multiple_of(D + d * rb, 16), rb), :]

    def gradients(p):
        take_wait(1, p)
        gs = g_all[p].reshape(T, D)
        term = dot(h_t[p], gs)

        @pl.when(p == 1)
        def _():
            up_b[...] = term.astype(BF16)
            up_copy(0).start()

        @pl.when(p == 0)
        def _():
            ob[0] = term

        for c in range(UNIT_CHUNKS):
            cols = pl.ds(c * uw, uw)
            d_hidden = dot_nt(gs, wb[p, cols, :])
            d_before = (d_hidden * dsl_all[p, :, cols]).astype(BF16)
            term = dot(n_t[p], d_before)

            @pl.when(p == 1)
            def _():
                up_a[:, cols] = term.astype(BF16)
                up_copy(1 + c).start()

            @pl.when(p == 0)
            def _():
                oa[0, :, cols] = term

    early = k0 < S // 4

    load(0, win, wa, p0).wait()
    load(1, wout, wb, p0).wait()

    @pl.when(k0 == 0)
    def _():
        feed_copy.wait()

    @pl.when(k0 > 0)
    def _():
        for c in range(HOP_CHUNKS):
            hop(0, p0, c).wait_recv()

    forward(p0, k0 < S)

    load(0, win, wa, p1).wait()
    load(1, wout, wb, p1).wait()

    @pl.when(early)
    def _():
        prepare(p0)

    for c in range(HOP_CHUNKS):
        hop(0, p1, c).wait_recv()
    forward(p1, k0 > 0)

    @pl.when(k0 >= S // 4)
    def _():
        prepare(p0)
        prepare(p1)

    @pl.when(k0 == 0)
    def _():
        g_all[p1, d] = (scale * h_out[p1].astype(F32)).astype(BF16)

    @pl.when(k0 > 0)
    def _():
        for c in range(HOP_CHUNKS):
            hop(1, p1, c).wait_recv()

    backward(p1)
    share_start(1, p1)

    @pl.when(early)
    def _():
        prepare(p1)

    @pl.when(k0 < half - 1)
    def _():
        gradients(p1)

    for c in range(HOP_CHUNKS):
        hop(1, p0, c).wait_recv()

    @pl.when(k0 > 0)
    def _():
        backward(p0)

    share_start(1, p0)

    @pl.when(k0 == half - 1)
    def _():
        gradients(p1)

    gradients(p0)

    up_copy(0).wait_recv()
    ob[0] = ob[0] + got_b[...].astype(F32)
    for c in range(UNIT_CHUNKS):
        cols = pl.ds(c * uw, uw)
        up_copy(1 + c).wait_recv()
        oa[0, :, cols] = oa[0, :, cols] + got_a[:, cols].astype(F32)

    for c in range(HOP_CHUNKS):
        hop(0, p0, c).wait_send()
        hop(1, p1, c).wait_send()

    @pl.when(k0 > 0)
    def _():
        for c in range(HOP_CHUNKS):
            hop(0, p1, c).wait_send()
            hop(1, p0, c).wait_send()

    for kind in range(2):
        for p in (p0, p1):
            for o in range(1, DP):
                share(kind, p, o).wait_send()
    for i in range(1 + UNIT_CHUNKS):
        up_copy(i).wait_send()


def per_device(feed, proj_in, proj_out):
    S, DP = lax.axis_size("section"), lax.axis_size("dp")
    micro, rows, D = feed.shape[1:]
    R = proj_in.shape[3]
    M, T = micro * rows, micro * rows * DP
    ra, rb = D // DP, R // DP
    scale = 8.0 / T
    aligned = ra % 128 == 0 and rb % 128 == 0
    vm = pltpu.VMEM
    dma = pltpu.SemaphoreType.DMA
    peers = max(DP - 1, 1)
    return pl.pallas_call(
        functools.partial(relay_kernel, S, DP, scale),
        out_shape=(
            jax.ShapeDtypeStruct((1, ra, R), F32),
            jax.ShapeDtypeStruct((1, rb, D), F32),
        ),
        in_specs=[pl.BlockSpec(memory_space=pl.ANY)] * 3,
        out_specs=(pl.BlockSpec(memory_space=pltpu.VMEM),) * 2,
        scratch_shapes=[
            vm((2, D, R), BF16),
            vm((2, R, D), BF16),
            vm((2, DP, M, D), BF16),
            vm((2, DP, M, D), BF16),
            vm((2, M, D), BF16),
            vm((2, M, D), BF16),
            vm((2, M, R), F32),
            vm((2, M, R), F32),
            vm((M, R), BF16),
            vm((M, R), BF16),
            vm((2, M, D), F32),
            vm((2, M, 128), F32),
            vm((2, ra, T), BF16),
            vm((2, rb, T), BF16),
            vm((2, T, R), F32),
            vm((ra, R), BF16),
            vm((rb, D), BF16),
            vm((ra, R), BF16),
            vm((rb, D), BF16),
            vm((16, 128) if aligned else (D + R, T), BF16),
            dma((2, 2)),
            dma(()),
            dma((2, 2, HOP_CHUNKS)),
            dma((2, 2, HOP_CHUNKS)),
            dma((2, 2, peers)),
            dma((2, 2, peers)),
            dma((1 + UNIT_CHUNKS,)),
            dma((1 + UNIT_CHUNKS,)),
        ],
        compiler_params=pltpu.CompilerParams(
            collective_id=0, has_side_effects=True, vmem_limit_bytes=60 * 1024 * 1024
        ),
        cost_estimate=pl.CostEstimate(
            flops=40 * M * D * R, bytes_accessed=16 * D * R, transcendentals=8 * T * R
        ),
    )(feed.reshape(2, M, D), proj_in, proj_out)


def solution(mesh):
    in_specs = (
        P(None, None, "dp", None),
        P(None, "section", None, None),
        P(None, "section", None, None),
    )
    out_specs = (P("section", "dp", None), P("section", "dp", None))
    return jax.shard_map(
        per_device, mesh=mesh, in_specs=in_specs, out_specs=out_specs, check_vma=False
    )
```

time: 604 us -> 79.9 us (0.13); the launches traced: 595 us -> 79.2 us
  matrix products: 145 us -> 0 us
  starting transfers between devices: 121 us -> 0 us
  blocking collectives: 89.8 us -> 0 us
  local copies, waits for them, and re-layouts: 92.9 us -> 4.13 us
  Pallas kernels: 0 us -> 74.4 us
  other arithmetic: 67.9 us -> 0 us
  waiting for transfers between devices: 62.6 us -> 0 us
  between operations: 14.2 us -> 0.64 us
    dot_general x92 -> x0, matrix products: 145 us -> none  [the longest x22 45.6 us: backward_section(): jnp.einsum('md,rd->mr', incoming, weight_out, preferred_element_type=jnp....]
    ppermute x40 -> x0, starting transfers between devices: 121 us -> none  [shifted(): lax.ppermute(value, axis, [(source, source + steps) for source in range(f...]
    all_to_all x2 -> x0, blocking collectives: 89.8 us -> none  [the longest x1 48.4 us: per_device(): lax.all_to_all(flat_up.astype(jnp.bfloat16), 'section', split_axis=1, con...]
    pallas_call x0 -> x1, Pallas kernels: none -> 74.4 us  [per_device(): pl.pallas_call(functools.partial(relay_kernel, S, DP, scale), out_shape=(...]
    reduce_scatter x2 -> x0, waiting for transfers between devices: 62.5 us -> none  [the longest x1 34.6 us: per_device(): lax.psum_scatter(paired_in.astype(jnp.bfloat16), 'dp', scatter_dimension=...]
    dynamic_update_slice x44 -> x0, other arithmetic: 38.5 us -> none  [store_slot(): lax.dynamic_update_index_in_dim(buffer, jnp.where(valid, value, old_value...]
    dynamic_slice x50 -> x0, local copies, waits for them, and re-layouts: 37.6 us -> none  [read_slot(): return lax.dynamic_index_in_dim(buffer, index, 0, keepdims=False)]
    slice x12 -> x0, local copies, waits for them, and re-layouts: 25.3 us -> none  [the longest x1 17.9 us: per_device(): paired_out = gout_down + returned[1].reshape(gout_down.shape)]
  transfers between devices with their start and end apart: 42 -> 0, of which waited for: 2 -> 0; matrix products, arithmetic and copies ran while one was open for 16% -> 0% of each run, Pallas kernels for 0% -> 0%
where the time goes in v1:
time: 79.9 us; the launch traced here: 79.2 us
  Pallas kernels  74.4 us (93%)
  local copies, waits for them, and re-layouts  4.13 us (5%)
    pallas_call x1, Pallas kernels, per_device(): pl.pallas_call(functools.partial(relay_kernel, S, DP, scale), out_shape=(...  74.4 us
    unnamed x2, local copies, waits for them, and re-layouts  4.13 us

profile of v1, /device:TPU:0, one launch (start us, length us, event | category | flops | bytes accessed | tf_op | source)
XLA Modules:
  0.0 79.2 jit_solution(14629410423210402783)
XLA Ops:
  0.6 74.4 %shard_map.50 = (f32[1,128,1536]{2,1,0:T(8,128)}, f32[1,384,512]{2,1,0:T(8,128)}) custom-call(bf16[2,64,512]{2,1,0:T(8,128)(2,1)} %bitcast.1, bf16[2,1,512,1536]{3,2,1,0:T(8,128)(2,1)} %win.1, bf16[2,1,1536,512]{3,2,1,0:T(8,128)(2,1)} %wout.1), custom_call_target="tpu_custom_call" | custom-call | flops 2013265920 | bytes 12582912 | tf_op jit(solution)/shard_map/pallas_call | solution.py:350
  75.1 2.1 %copy.7 = f32[1,128,1536]{2,1,0:T(8,128)} copy(f32[1,128,1536]{2,1,0:T(8,128)} %get-tuple-element.4) | data formatting | bytes 1572864
  77.1 2.1 %copy.8 = f32[1,384,512]{2,1,0:T(8,128)} copy(f32[1,384,512]{2,1,0:T(8,128)} %get-tuple-element.5) | data formatting | bytes 1572864

commit v2 on v1

v2 whole, which is shorter than its diff:
```python
import functools

import jax
import jax.numpy as jnp
from jax import lax
from jax.experimental import pallas as pl
from jax.experimental.pallas import tpu as pltpu
from jax.sharding import PartitionSpec as P

MESH = pl.DeviceIdType.MESH
F32, BF16 = jnp.float32, jnp.bfloat16
HOP_CHUNKS = 2
UNIT_CHUNKS = 3


def dot(a, b):
    return jnp.dot(a, b, preferred_element_type=F32)


def dot_nt(a, b):
    return lax.dot_general(a, b, (((1,), (1,)), ((), ())), preferred_element_type=F32)


def sigmoid(x):
    return 0.5 + 0.5 * jnp.tanh(0.5 * x)


def norm_factor(wide):
    return lax.rsqrt(jnp.mean(wide * wide, axis=-1, keepdims=True) + 1e-05)


def relay_kernel(
    S, DP, scale,
    feed, win, wout, oa, ob,
    wa, wb, h_all, g_all, h_out, g_out, pre_own, dsl_own, hid_own, dpre_own, u_own, r_own,
    n_t, h_t, dsl_all, up_a, up_b, got_a, got_b, own_a, own_b, dh_own, full_t,
    load_sem, feed_sem, hop_send, hop_recv, all_send, all_recv, up_send, up_recv,
):
    s, d = lax.axis_index("section"), lax.axis_index("dp")
    M, D = h_all.shape[2], h_all.shape[3]
    R = wa.shape[2]
    T = DP * M
    ra, rb = D // DP, R // DP
    half = S // 2
    p0 = s // half
    p1 = 1 - p0
    k0 = s + p0 * (S - 1 - 2 * s)
    mirror = S - 1 - s
    cw, uw = D // HOP_CHUNKS, R // UNIT_CHUNKS

    def unit_cols(c):
        return pl.ds(pl.multiple_of(c * uw, uw), uw)

    def load(i, src, dst, p):
        return pltpu.make_async_copy(src.at[p, 0], dst.at[p], load_sem.at[i, p])

    feed_copy = pltpu.make_async_copy(feed.at[p0], h_all.at[p0, d], feed_sem)

    @pl.when(k0 == 0)
    def _():
        feed_copy.start()

    for p in (p0, p1):
        load(0, win, wa, p).start()
        load(1, wout, wb, p).start()

    barrier = pltpu.get_barrier_semaphore()
    for other in (lax.rem(s + 1, S), lax.rem(s + S - 1, S), mirror):
        pl.semaphore_signal(barrier, inc=1, device_id={"section": other}, device_id_type=MESH)
    for o in range(1, DP):
        pl.semaphore_signal(
            barrier, inc=1, device_id={"dp": lax.rem(d + o, DP)}, device_id_type=MESH
        )
    pl.semaphore_wait(barrier, 3 + DP - 1)

    def hop(kind, p, c):
        step = 1 - 2 * p
        peer = s + step if kind == 0 else s - step
        src, dst = (h_out, h_all) if kind == 0 else (g_out, g_all)
        cols = pl.ds(c * cw, cw)
        return pltpu.make_async_remote_copy(
            src_ref=src.at[p, :, cols],
            dst_ref=dst.at[p, d, :, cols],
            send_sem=hop_send.at[kind, p, c],
            recv_sem=hop_recv.at[kind, p, c],
            device_id={"section": peer},
            device_id_type=MESH,
        )

    def share(kind, p, o):
        buf = h_all if kind == 0 else g_all
        return pltpu.make_async_remote_copy(
            src_ref=buf.at[p, d],
            dst_ref=buf.at[p, d],
            send_sem=all_send.at[kind, p, o - 1],
            recv_sem=all_recv.at[kind, p, o - 1],
            device_id={"dp": lax.rem(d + o, DP)},
            device_id_type=MESH,
        )

    def take(kind, p, o):
        buf = h_all if kind == 0 else g_all
        source = lax.rem(d + DP - o, DP)
        return pltpu.make_async_remote_copy(
            src_ref=buf.at[p, source],
            dst_ref=buf.at[p, source],
            send_sem=all_send.at[kind, p, o - 1],
            recv_sem=all_recv.at[kind, p, o - 1],
            device_id={"dp": source},
            device_id_type=MESH,
        )

    def share_start(kind, p):
        for o in range(1, DP):
            share(kind, p, o).start()

    def take_wait(kind, p):
        for o in range(1, DP):
            take(kind, p, o).wait_recv()

    def up_copy_b():
        return pltpu.make_async_remote_copy(
            src_ref=up_b,
            dst_ref=got_b,
            send_sem=up_send.at[0],
            recv_sem=up_recv.at[0],
            device_id={"section": mirror},
            device_id_type=MESH,
        )

    def up_copy_a(c):
        cols = unit_cols(c)
        return pltpu.make_async_remote_copy(
            src_ref=up_a.at[:, cols],
            dst_ref=got_a.at[:, cols],
            send_sem=up_send.at[1 + c],
            recv_sem=up_recv.at[1 + c],
            device_id={"section": mirror},
            device_id_type=MESH,
        )

    def forward(p, k):
        load(0, win, wa, p).wait()

        @pl.when(k == 0)
        def _():
            feed_copy.wait()

        squares = jnp.zeros((M, 1), F32)
        for c in range(HOP_CHUNKS):
            part = pl.ds(c * cw, cw)

            @pl.when(k > 0)
            def _():
                hop(0, p, c).wait_recv()

            piece = h_all[p, d, :, part]
            wide = piece.astype(F32)
            squares += jnp.sum(wide * wide, axis=-1, keepdims=True)
            last = c == HOP_CHUNKS - 1
            if last:
                factor = lax.rsqrt(squares * (1.0 / D) + 1e-05)
            for u in range(UNIT_CHUNKS):
                cols = pl.ds(u * uw, uw)
                before = dot(piece, wa[p, part, cols])
                if c:
                    before += pre_own[p, :, cols]
                if last:
                    before *= factor
                    hid_own[:, cols] = (before * sigmoid(before)).astype(BF16)
                pre_own[p, :, cols] = before
        load(1, wout, wb, p).wait()
        for c in range(HOP_CHUNKS):
            cols = pl.ds(c * cw, cw)
            old = h_all[p, d, :, cols].astype(F32)
            h_out[p, :, cols] = (old + dot(hid_own[...], wb[p, :, cols])).astype(BF16)

            @pl.when(k < S - 1)
            def _():
                hop(0, p, c).start()

        share_start(0, p)
        u_own[p] = h_all[p, d].astype(F32) * factor
        r_own[p] = jnp.broadcast_to(factor, (M, 128))
        for u in range(UNIT_CHUNKS):
            cols = pl.ds(u * uw, uw)
            before = pre_own[p, :, cols]
            sigma = sigmoid(before)
            dsl_own[p, :, cols] = sigma * (1.0 + before * (1.0 - sigma))

    def backward(p, k):
        @pl.when(k == S - 1)
        def _():
            g_all[p, d] = (scale * h_out[p].astype(F32)).astype(BF16)

        @pl.when(k == 0)
        def _():
            for c in range(HOP_CHUNKS):
                hop(1, p, c).wait_recv()
            share_start(1, p)

        @pl.when(k > 0)
        def _():
            total = jnp.zeros((M, 1), F32)
            for c in range(HOP_CHUNKS):
                part = pl.ds(c * cw, cw)

                @pl.when(k < S - 1)
                def _():
                    hop(1, p, c).wait_recv()

                piece = g_all[p, d, :, part]
                for u in range(UNIT_CHUNKS):
                    cols = pl.ds(u * uw, uw)
                    d_hidden = dot_nt(piece, wb[p, cols, part])
                    if c:
                        d_hidden += dh_own[:, cols]
                    if c < HOP_CHUNKS - 1:
                        dh_own[:, cols] = d_hidden
                    else:
                        d_before = (d_hidden * dsl_own[p, :, cols]).astype(BF16)
                        dpre_own[:, cols] = d_before
                        total += jnp.sum(
                            d_before.astype(F32) * pre_own[p, :, cols], axis=-1, keepdims=True
                        )
            mean = total * (1.0 / D)
            factor = r_own[p, :, 0:1]
            for c in range(HOP_CHUNKS):
                cols = pl.ds(c * cw, cw)
                d_normed = dot_nt(dpre_own[...], wa[p, cols, :])
                out = g_all[p, d, :, cols].astype(F32) + factor * (
                    d_normed - u_own[p, :, cols] * mean
                )
                g_out[p, :, cols] = out.astype(BF16)
                hop(1, p, c).start()
            share_start(1, p)

    aligned = ra % 128 == 0 and rb % 128 == 0
    block = min(T, 256)

    def prepare(p):
        take_wait(0, p)

        def rows_step(b):
            per = block // M
            rows = pl.ds(pl.multiple_of(b * block, block), block)
            wide = h_all[p, pl.ds(b * per, per)].reshape(block, D).astype(F32)
            factor = norm_factor(wide)
            normed_wide = wide * factor
            normed = normed_wide.astype(BF16)
            if aligned:
                mine = h_all[
                    p, pl.ds(b * per, per), :, pl.ds(pl.multiple_of(d * ra, 128), ra)
                ].reshape(block, ra).astype(F32) * factor
                n_t[p, :, rows] = mine.T.astype(BF16)
                before = dot(normed, wa[p, :, pl.ds(pl.multiple_of(d * rb, 128), rb)])
                h_t[p, :, rows] = (before * sigmoid(before)).T.astype(BF16)
            else:
                full_t[0:D, rows] = normed_wide.T.astype(BF16)

            @pl.loop(0, UNIT_CHUNKS)
            def _(c):
                cols = unit_cols(c)
                before = dot(normed, wa[p, :, cols])
                sigma = sigmoid(before)
                dsl_all[p, rows, cols] = sigma * (1.0 + before * (1.0 - sigma))
                if not aligned:
                    full_t[pl.ds(pl.multiple_of(D + c * uw, 16), uw), rows] = (
                        (before * sigma).T.astype(BF16)
                    )

        if T == block:
            rows_step(0)
        else:
            pl.loop(0, T // block)(rows_step)
        if not aligned:
            n_t[p] = full_t[pl.ds(pl.multiple_of(d * ra, 16), ra), :]
            h_t[p] = full_t[pl.ds(pl.multiple_of(D + d * rb, 16), rb), :]

    def gradients(p):
        take_wait(1, p)
        gs = g_all[p].reshape(T, D)
        term = dot(h_t[p], gs)

        @pl.when(p == 1)
        def _():
            up_b[...] = term.astype(BF16)
            up_copy_b().start()

        @pl.when(p == 0)
        def _():
            own_b[...] = term

        @pl.loop(0, UNIT_CHUNKS)
        def _(c):
            cols = unit_cols(c)
            d_hidden = dot_nt(g_all[p].reshape(T, D), wb[p, cols, :])
            d_before = (d_hidden * dsl_all[p, :, cols]).astype(BF16)
            term = dot(n_t[p], d_before)

            @pl.when(p == 1)
            def _():
                up_a[:, cols] = term.astype(BF16)
                up_copy_a(c).start()

            @pl.when(p == 0)
            def _():
                own_a[:, cols] = term

    early = (k0 < S // 4).astype(jnp.int32)
    middle = (k0 == half - 1).astype(jnp.int32)

    @pl.loop(0, 4)
    def _(j):
        q = lax.rem((j + 1) // 2, 2)
        p = p0 + q * (1 - 2 * p0)
        k = k0 + q * (S - 1 - 2 * k0)

        @pl.when(j < 2)
        def _():
            forward(p, k)

        @pl.when(j >= 2)
        def _():
            backward(p, k)

        is1 = (j == 1).astype(jnp.int32)
        is2 = (j == 2).astype(jnp.int32)
        is3 = (j == 3).astype(jnp.int32)
        first = early * is2
        count = early * (1 - is1 - is3) + (1 - early) * 2 * is1

        @pl.loop(0, count)
        def _(i):
            prepare(p0 + (first + i) * (1 - 2 * p0))

        count = is2 * (1 - middle) + is3 * (1 + middle)

        @pl.loop(0, count)
        def _(i):
            which = is2 + is3 * (middle - i)
            gradients(p0 + which * (1 - 2 * p0))

    up_copy_b().wait_recv()
    ob[...] = (own_b[...] + got_b[...].astype(F32)).astype(BF16)
    for c in range(UNIT_CHUNKS):
        cols = pl.ds(c * uw, uw)
        up_copy_a(c).wait_recv()
        oa[:, cols] = (own_a[:, cols] + got_a[:, cols].astype(F32)).astype(BF16)

    for c in range(HOP_CHUNKS):
        hop(0, p0, c).wait_send()
        hop(1, p1, c).wait_send()

    @pl.when(k0 > 0)
    def _():
        for c in range(HOP_CHUNKS):
            hop(0, p1, c).wait_send()
            hop(1, p0, c).wait_send()

    for kind in range(2):
        for p in (p0, p1):
            for o in range(1, DP):
                share(kind, p, o).wait_send()
    up_copy_b().wait_send()
    for c in range(UNIT_CHUNKS):
        up_copy_a(c).wait_send()


def per_device(feed, proj_in, proj_out):
    S, DP = lax.axis_size("section"), lax.axis_size("dp")
    micro, rows, D = feed.shape[1:]
    R = proj_in.shape[3]
    M, T = micro * rows, micro * rows * DP
    ra, rb = D // DP, R // DP
    scale = 8.0 / T
    aligned = ra % 128 == 0 and rb % 128 == 0
    vm = pltpu.VMEM
    dma = pltpu.SemaphoreType.DMA
    peers = max(DP - 1, 1)
    grad_a, grad_b = pl.pallas_call(
        functools.partial(relay_kernel, S, DP, scale),
        out_shape=(
            jax.ShapeDtypeStruct((ra, R), BF16),
            jax.ShapeDtypeStruct((rb, D), BF16),
        ),
        in_specs=[pl.BlockSpec(memory_space=pltpu.HBM)] * 3,
        out_specs=(pl.BlockSpec(memory_space=pltpu.VMEM),) * 2,
        scratch_shapes=[
            vm((2, D, R), BF16),
            vm((2, R, D), BF16),
            vm((2, DP, M, D), BF16),
            vm((2, DP, M, D), BF16),
            vm((2, M, D), BF16),
            vm((2, M, D), BF16),
            vm((2, M, R), F32),
            vm((2, M, R), F32),
            vm((M, R), BF16),
            vm((M, R), BF16),
            vm((2, M, D), F32),
            vm((2, M, 128), F32),
            vm((2, ra, T), BF16),
            vm((2, rb, T), BF16),
            vm((2, T, R), F32),
            vm((ra, R), BF16),
            vm((rb, D), BF16),
            vm((ra, R), BF16),
            vm((rb, D), BF16),
            vm((ra, R), F32),
            vm((rb, D), F32),
            vm((M, R), F32),
            vm((16, 128) if aligned else (D + R, T), BF16),
            dma((2, 2)),
            dma(()),
            dma((2, 2, HOP_CHUNKS)),
            dma((2, 2, HOP_CHUNKS)),
            dma((2, 2, peers)),
            dma((2, 2, peers)),
            dma((1 + UNIT_CHUNKS,)),
            dma((1 + UNIT_CHUNKS,)),
        ],
        compiler_params=pltpu.CompilerParams(
            collective_id=0, has_side_effects=True, vmem_limit_bytes=60 * 1024 * 1024
        ),
        cost_estimate=pl.CostEstimate(
            flops=40 * M * D * R, bytes_accessed=16 * D * R, transcendentals=8 * T * R
        ),
    )(feed.reshape(2, M, D), proj_in, proj_out)
    return grad_a.astype(F32)[None], grad_b.astype(F32)[None]


def solution(mesh):
    in_specs = (
        P(None, None, "dp", None),
        P(None, "section", None, None),
        P(None, "section", None, None),
    )
    out_specs = (P("section", "dp", None), P("section", "dp", None))
    return jax.shard_map(
        per_device, mesh=mesh, in_specs=in_specs, out_specs=out_specs, check_vma=False
    )
```

time: 79.9 us -> 77.9 us (0.975)
  local copies, waits for them, and re-layouts: 4.13 us -> 0 us
  other arithmetic: 0 us -> 3.92 us
  Pallas kernels: 74.4 us -> 72.7 us
    unnamed x2 -> x0, local copies, waits for them, and re-layouts: 4.13 us -> none
    broadcast_in_dim x0 -> x2, other arithmetic: none -> 3.92 us  [per_device(): return (grad_a.astype(F32)[None], grad_b.astype(F32)[None])]
    pallas_call x1, Pallas kernels: 74.4 us -> 72.7 us  [per_device(): pl.pallas_call(functools.partial(relay_kernel, S, DP, scale), out_shape=(...]
where the time goes in v2:
time: 77.9 us; the launch traced here: 77.3 us
  Pallas kernels  72.7 us (93%)
  other arithmetic  3.92 us (5%)
    pallas_call x1, Pallas kernels, per_device(): pl.pallas_call(functools.partial(relay_kernel, S, DP, scale), out_shape=(...  72.7 us
    broadcast_in_dim x2, other arithmetic, per_device(): return (grad_a.astype(F32)[None], grad_b.astype(F32)[None])  3.92 us

profile of v2, /device:TPU:0, one launch (start us, length us, event | category | flops | bytes accessed | tf_op | source)
XLA Modules:
  0.0 77.3 jit_solution(5843323017295479041)
XLA Ops:
  0.6 72.7 %shard_map.50 = (bf16[128,1536]{1,0:T(8,128)(2,1)}, bf16[384,512]{1,0:T(8,128)(2,1)}) custom-call(bf16[2,64,512]{2,1,0:T(8,128)(2,1)} %bitcast.7, bf16[2,1,512,1536]{3,2,1,0:T(8,128)(2,1)} %win.1, bf16[2,1,1536,512]{3,2,1,0:T(8,128)(2,1)} %wout.1), custom_call_target="tpu_custom_call" | custom-call | flops 2013265920 | bytes 12582912 | tf_op jit(solution)/shard_map/pallas_call | solution.py:381
  73.4 2.0 %bitcast_convert_fusion.1 = f32[1,128,1536]{2,1,0:T(8,128)} fusion(bf16[128,1536]{1,0:T(8,128)(2,1)} %get-tuple-element.4), kind=kLoop, calls=%fused_computation.1 | loop fusion | flops 196608 | bytes 1179648 | tf_op jit(solution)/shard_map/broadcast_in_dim | solution.py:429
  75.3 2.0 %bitcast_convert_fusion = f32[1,384,512]{2,1,0:T(8,128)} fusion(bf16[384,512]{1,0:T(8,128)(2,1)} %get-tuple-element.5), kind=kLoop, calls=%fused_computation | loop fusion | flops 196608 | bytes 1179648 | tf_op jit(solution)/shard_map/broadcast_in_dim | solution.py:429

commit v3 on v2

--- a/solution.py
+++ b/solution.py
@@ -11,6 +11,8 @@
 F32, BF16 = jnp.float32, jnp.bfloat16
 HOP_CHUNKS = 2
 UNIT_CHUNKS = 3
+GRAD_CHUNKS = 2
+PIECES = 4
 
 
 def dot(a, b):
@@ -33,8 +35,8 @@
     S, DP, scale,
     feed, win, wout, oa, ob,
     wa, wb, h_all, g_all, h_out, g_out, pre_own, dsl_own, hid_own, dpre_own, u_own, r_own,
-    n_t, h_t, dsl_all, up_a, up_b, got_a, got_b, own_a, own_b, dh_own, full_t,
-    load_sem, feed_sem, hop_send, hop_recv, all_send, all_recv, up_send, up_recv,
+    n_t, h_t, dsl_all, up_a, up_b, got_a, got_b, own_a, own_b, dh_own, via_a, via_b, full_t,
+    load_sem, feed_sem, hop_send, hop_recv, all_send, all_recv, up_send, up_recv, via_send, via_recv,
 ):
     s, d = lax.axis_index("section"), lax.axis_index("dp")
     M, D = h_all.shape[2], h_all.shape[3]
@@ -46,6 +48,8 @@
     p1 = 1 - p0
     k0 = s + p0 * (S - 1 - 2 * s)
     mirror = S - 1 - s
+    flip = s + 2 * (1 - 2 * lax.rem(s // 2, 2))
+    cross = S - 1 - flip
     cw, uw = D // HOP_CHUNKS, R // UNIT_CHUNKS
 
     def unit_cols(c):
@@ -65,13 +69,13 @@
         load(1, wout, wb, p).start()
 
     barrier = pltpu.get_barrier_semaphore()
-    for other in (lax.rem(s + 1, S), lax.rem(s + S - 1, S), mirror):
+    for other in (lax.rem(s + 1, S), lax.rem(s + S - 1, S), mirror, flip, cross):
         pl.semaphore_signal(barrier, inc=1, device_id={"section": other}, device_id_type=MESH)
     for o in range(1, DP):
         pl.semaphore_signal(
             barrier, inc=1, device_id={"dp": lax.rem(d + o, DP)}, device_id_type=MESH
         )
-    pl.semaphore_wait(barrier, 3 + DP - 1)
+    pl.semaphore_wait(barrier, 5 + DP - 1)
 
     def hop(kind, p, c):
         step = 1 - 2 * p
@@ -118,26 +122,49 @@
         for o in range(1, DP):
             take(kind, p, o).wait_recv()
 
-    def up_copy_b():
+    def piece_of(i, b_ref, a_ref):
+        if i < PIECES:
+            return b_ref.at[:, pl.ds(i * (D // PIECES), D // PIECES)]
+        return a_ref.at[:, pl.ds((i - PIECES) * (R // PIECES), R // PIECES)]
+
+    def up_copy(i):
         return pltpu.make_async_remote_copy(
-            src_ref=up_b,
-            dst_ref=got_b,
-            send_sem=up_send.at[0],
-            recv_sem=up_recv.at[0],
+            src_ref=piece_of(i, up_b, up_a),
+            dst_ref=piece_of(i, got_b, got_a),
+            send_sem=up_send.at[i],
+            recv_sem=up_recv.at[i],
             device_id={"section": mirror},
             device_id_type=MESH,
         )
 
-    def up_copy_a(c):
-        cols = unit_cols(c)
+    def via_copy(i):
         return pltpu.make_async_remote_copy(
-            src_ref=up_a.at[:, cols],
-            dst_ref=got_a.at[:, cols],
-            send_sem=up_send.at[1 + c],
-            recv_sem=up_recv.at[1 + c],
-            device_id={"section": mirror},
+            src_ref=piece_of(i, up_b, up_a),
+            dst_ref=piece_of(i, via_b, via_a),
+            send_sem=up_send.at[i],
+            recv_sem=via_recv.at[i],
+            device_id={"section": flip if i % 2 == 0 else cross},
             device_id_type=MESH,
         )
+
+    def onward_copy(i):
+        return pltpu.make_async_remote_copy(
+            src_ref=piece_of(i, via_b, via_a),
+            dst_ref=piece_of(i, got_b, got_a),
+            send_sem=via_send.at[i],
+            recv_sem=up_recv.at[i],
+            device_id={"section": cross if i % 2 == 0 else flip},
+            device_id_type=MESH,
+        )
+
+    def send_up(i):
+        @pl.when(s >= S - S // 4)
+        def _():
+            via_copy(i).start()
+
+        @pl.when(s < S - S // 4)
+        def _():
+            up_copy(i).start()
 
     def forward(p, k):
         load(0, win, wa, p).wait()
@@ -279,21 +306,21 @@
 
     def gradients(p):
         take_wait(1, p)
-        gs = g_all[p].reshape(T, D)
-        term = dot(h_t[p], gs)
+        term = dot(h_t[p], g_all[p].reshape(T, D))
 
         @pl.when(p == 1)
         def _():
             up_b[...] = term.astype(BF16)
-            up_copy_b().start()
+            for i in range(PIECES):
+                send_up(i)
 
         @pl.when(p == 0)
         def _():
             own_b[...] = term
 
-        @pl.loop(0, UNIT_CHUNKS)
-        def _(c):
-            cols = unit_cols(c)
+        gw = R // GRAD_CHUNKS
+        for c in range(GRAD_CHUNKS):
+            cols = pl.ds(c * gw, gw)
             d_hidden = dot_nt(g_all[p].reshape(T, D), wb[p, cols, :])
             d_before = (d_hidden * dsl_all[p, :, cols]).astype(BF16)
             term = dot(n_t[p], d_before)
@@ -301,7 +328,9 @@
             @pl.when(p == 1)
             def _():
                 up_a[:, cols] = term.astype(BF16)
-                up_copy_a(c).start()
+                per = PIECES // GRAD_CHUNKS
+                for i in range(per):
+                    send_up(PIECES + c * per + i)
 
             @pl.when(p == 0)
             def _():
@@ -341,12 +370,20 @@
             which = is2 + is3 * (middle - i)
             gradients(p0 + which * (1 - 2 * p0))
 
-    up_copy_b().wait_recv()
-    ob[...] = (own_b[...] + got_b[...].astype(F32)).astype(BF16)
-    for c in range(UNIT_CHUNKS):
-        cols = pl.ds(c * uw, uw)
-        up_copy_a(c).wait_recv()
-        oa[:, cols] = (own_a[:, cols] + got_a[:, cols].astype(F32)).astype(BF16)
+    for lead, on_route in ((0, flip >= S - S // 4), (1, cross >= S - S // 4)):
+
+        @pl.when(on_route)
+        def _():
+            for i in range(lead, 2 * PIECES, 2):
+                via_copy(i).wait_recv()
+                onward_copy(i).start()
+
+    for i in range(2 * PIECES):
+        up_copy(i).wait_recv()
+        out, own, got = (ob, own_b, got_b) if i < PIECES else (oa, own_a, got_a)
+        width = (D if i < PIECES else R) // PIECES
+        cols = pl.ds((i % PIECES) * width, width)
+        out[:, cols] = (own[:, cols] + got[:, cols].astype(F32)).astype(BF16)
 
     for c in range(HOP_CHUNKS):
         hop(0, p0, c).wait_send()
@@ -362,9 +399,41 @@
         for p in (p0, p1):
             for o in range(1, DP):
                 share(kind, p, o).wait_send()
-    up_copy_b().wait_send()
-    for c in range(UNIT_CHUNKS):
-        up_copy_a(c).wait_send()
+    for i in range(2 * PIECES):
+        up_copy(i).wait_send()
+    for lead, on_route in ((0, flip >= S - S // 4), (1, cross >= S - S // 4)):
+
+        @pl.when(on_route)
+        def _():
+            for i in range(lead, 2 * PIECES, 2):
+                onward_copy(i).wait_send()
+
+
+def widen_kernel(a_ref, b_ref, oa_ref, ob_ref):
+    oa_ref[0] = a_ref[...].astype(F32)
+    ob_ref[0] = b_ref[...].astype(F32)
+
+
+def widen(a, b):
+    parts = 2
+
+    def narrow(x):
+        return pl.BlockSpec((x.shape[0], x.shape[1] // parts), lambda i: (0, i))
+
+    def wide(x):
+        return pl.BlockSpec((1, x.shape[0], x.shape[1] // parts), lambda i: (0, 0, i))
+
+    return pl.pallas_call(
+        widen_kernel,
+        grid=(parts,),
+        out_shape=tuple(jax.ShapeDtypeStruct((1,) + x.shape, F32) for x in (a, b)),
+        in_specs=[narrow(a), narrow(b)],
+        out_specs=(wide(a), wide(b)),
+        compiler_params=pltpu.CompilerParams(vmem_limit_bytes=60 * 1024 * 1024),
+        cost_estimate=pl.CostEstimate(
+            flops=a.size + b.size, bytes_accessed=6 * (a.size + b.size), transcendentals=0
+        ),
+    )(a, b)
 
 
 def per_device(feed, proj_in, proj_out):
@@ -409,6 +478,8 @@
             vm((ra, R), F32),
             vm((rb, D), F32),
             vm((M, R), F32),
+            vm((ra, R), BF16),
+            vm((rb, D), BF16),
             vm((16, 128) if aligned else (D + R, T), BF16),
             dma((2, 2)),
             dma(()),
@@ -416,8 +487,10 @@
             dma((2, 2, HOP_CHUNKS)),
             dma((2, 2, peers)),
             dma((2, 2, peers)),
-            dma((1 + UNIT_CHUNKS,)),
-            dma((1 + UNIT_CHUNKS,)),
+            dma((2 * PIECES,)),
+            dma((2 * PIECES,)),
+            dma((2 * PIECES,)),
+            dma((2 * PIECES,)),
         ],
         compiler_params=pltpu.CompilerParams(
             collective_id=0, has_side_effects=True, vmem_limit_bytes=60 * 1024 * 1024
@@ -426,7 +499,7 @@
             flops=40 * M * D * R, bytes_accessed=16 * D * R, transcendentals=8 * T * R
         ),
     )(feed.reshape(2, M, D), proj_in, proj_out)
-    return grad_a.astype(F32)[None], grad_b.astype(F32)[None]
+    return widen(grad_a, grad_b)
 
 
 def solution(mesh):

time: 77.9 us -> 82 us (1.053)
  Pallas kernels: 72.7 us -> 81.2 us
  other arithmetic: 3.92 us -> 0 us
    pallas_call x1, Pallas kernels: 72.7 us -> 79 us  [per_device(): pl.pallas_call(functools.partial(relay_kernel, S, DP, scale), out_shape=(...]
    broadcast_in_dim x2 -> x0, other arithmetic: 3.92 us -> none  [per_device(): return (grad_a.astype(F32)[None], grad_b.astype(F32)[None])]
    pallas_call x0 -> x1, Pallas kernels: none -> 2.2 us  [widen(): pl.pallas_call(widen_kernel, grid=(parts,), out_shape=tuple((jax.ShapeDty...]
where the time goes in v3:
time: 82 us; the launch traced here: 81.9 us
  Pallas kernels  81.2 us (99%)
    pallas_call x1, Pallas kernels, per_device(): pl.pallas_call(functools.partial(relay_kernel, S, DP, scale), out_shape=(...  79 us
    pallas_call x1, Pallas kernels, widen(): pl.pallas_call(widen_kernel, grid=(parts,), out_shape=tuple((jax.ShapeDty...  2.2 us

profile of v3, /device:TPU:0, one launch (start us, length us, event | category | flops | bytes accessed | tf_op | source)
XLA Modules:
  0.0 81.9 jit_solution(12647263659819623623)
XLA Ops:
  0.6 79.0 %shard_map.50 = (bf16[128,1536]{1,0:T(8,128)(2,1)}, bf16[384,512]{1,0:T(8,128)(2,1)}) custom-call(bf16[2,64,512]{2,1,0:T(8,128)(2,1)} %bitcast.1, bf16[2,1,512,1536]{3,2,1,0:T(8,128)(2,1)} %win.1, bf16[2,1,1536,512]{3,2,1,0:T(8,128)(2,1)} %wout.1), custom_call_target="tpu_custom_call" | custom-call | flops 2013265920 | bytes 12582912 | tf_op jit(solution)/shard_map/pallas_call | solution.py:450
  79.7 2.2 %shard_map.51 = (f32[1,128,1536]{2,1,0:T(8,128)}, f32[1,384,512]{2,1,0:T(8,128)}) custom-call(bf16[128,1536]{1,0:T(8,128)(2,1)} %get-tuple-element.4.a_ref, bf16[384,512]{1,0:T(8,128)(2,1)} %get-tuple-element.5.b_ref), custom_call_target="tpu_custom_call" | custom-call | flops 393216 | bytes 2359296 | tf_op jit(solution)/shard_map/pallas_call | solution.py:426

commit v4 on v2

--- a/solution.py
+++ b/solution.py
@@ -11,6 +11,7 @@
 F32, BF16 = jnp.float32, jnp.bfloat16
 HOP_CHUNKS = 2
 UNIT_CHUNKS = 3
+GRAD_CHUNKS = 3
 
 
 def dot(a, b):
@@ -33,8 +34,8 @@
     S, DP, scale,
     feed, win, wout, oa, ob,
     wa, wb, h_all, g_all, h_out, g_out, pre_own, dsl_own, hid_own, dpre_own, u_own, r_own,
-    n_t, h_t, dsl_all, up_a, up_b, got_a, got_b, own_a, own_b, dh_own, full_t,
-    load_sem, feed_sem, hop_send, hop_recv, all_send, all_recv, up_send, up_recv,
+    n_t, h_t, dsl_all, up_a, got_a, own_a, hm_t, dh_own, full_t,
+    load_sem, feed_sem, hop_send, hop_recv, all_send, all_recv, up_send, up_recv, pair_send, pair_recv,
 ):
     s, d = lax.axis_index("section"), lax.axis_index("dp")
     M, D = h_all.shape[2], h_all.shape[3]
@@ -60,9 +61,8 @@
     def _():
         feed_copy.start()
 
-    for p in (p0, p1):
-        load(0, win, wa, p).start()
-        load(1, wout, wb, p).start()
+    load(0, win, wa, p0).start()
+    load(1, wout, wb, p0).start()
 
     barrier = pltpu.get_barrier_semaphore()
     for other in (lax.rem(s + 1, S), lax.rem(s + S - 1, S), mirror):
@@ -72,6 +72,9 @@
             barrier, inc=1, device_id={"dp": lax.rem(d + o, DP)}, device_id_type=MESH
         )
     pl.semaphore_wait(barrier, 3 + DP - 1)
+
+    load(0, win, wa, p1).start()
+    load(1, wout, wb, p1).start()
 
     def hop(kind, p, c):
         step = 1 - 2 * p
@@ -118,26 +121,27 @@
         for o in range(1, DP):
             take(kind, p, o).wait_recv()
 
-    def up_copy_b():
+    gw = R // GRAD_CHUNKS
+
+    def to_mirror(src, dst, send_sem, recv_sem):
         return pltpu.make_async_remote_copy(
-            src_ref=up_b,
-            dst_ref=got_b,
-            send_sem=up_send.at[0],
-            recv_sem=up_recv.at[0],
+            src_ref=src,
+            dst_ref=dst,
+            send_sem=send_sem,
+            recv_sem=recv_sem,
             device_id={"section": mirror},
             device_id_type=MESH,
         )
 
-    def up_copy_a(c):
-        cols = unit_cols(c)
-        return pltpu.make_async_remote_copy(
-            src_ref=up_a.at[:, cols],
-            dst_ref=got_a.at[:, cols],
-            send_sem=up_send.at[1 + c],
-            recv_sem=up_recv.at[1 + c],
-            device_id={"section": mirror},
-            device_id_type=MESH,
-        )
+    def up_copy(c):
+        cols = pl.ds(c * gw, gw)
+        return to_mirror(up_a.at[:, cols], got_a.at[:, cols], up_send.at[c], up_recv.at[c])
+
+    def hidden_copy():
+        return to_mirror(h_t.at[1], hm_t, pair_send.at[0], pair_recv.at[0])
+
+    def seed_copy():
+        return to_mirror(g_all.at[1, d], g_all.at[2, d], pair_send.at[1], pair_recv.at[1])
 
     def forward(p, k):
         load(0, win, wa, p).wait()
@@ -188,6 +192,11 @@
             sigma = sigmoid(before)
             dsl_own[p, :, cols] = sigma * (1.0 + before * (1.0 - sigma))
 
+    def seed_start(p):
+        @pl.when(p == 1)
+        def _():
+            seed_copy().start()
+
     def backward(p, k):
         @pl.when(k == S - 1)
         def _():
@@ -197,6 +206,7 @@
         def _():
             for c in range(HOP_CHUNKS):
                 hop(1, p, c).wait_recv()
+            seed_start(p)
             share_start(1, p)
 
         @pl.when(k > 0)
@@ -233,6 +243,7 @@
                 )
                 g_out[p, :, cols] = out.astype(BF16)
                 hop(1, p, c).start()
+            seed_start(p)
             share_start(1, p)
 
     aligned = ra % 128 == 0 and rb % 128 == 0
@@ -277,23 +288,14 @@
             n_t[p] = full_t[pl.ds(pl.multiple_of(d * ra, 16), ra), :]
             h_t[p] = full_t[pl.ds(pl.multiple_of(D + d * rb, 16), rb), :]
 
+        @pl.when(p == 1)
+        def _():
+            hidden_copy().start()
+
     def gradients(p):
         take_wait(1, p)
-        gs = g_all[p].reshape(T, D)
-        term = dot(h_t[p], gs)
-
-        @pl.when(p == 1)
-        def _():
-            up_b[...] = term.astype(BF16)
-            up_copy_b().start()
-
-        @pl.when(p == 0)
-        def _():
-            own_b[...] = term
-
-        @pl.loop(0, UNIT_CHUNKS)
-        def _(c):
-            cols = unit_cols(c)
+        for c in range(GRAD_CHUNKS):
+            cols = pl.ds(c * gw, gw)
             d_hidden = dot_nt(g_all[p].reshape(T, D), wb[p, cols, :])
             d_before = (d_hidden * dsl_all[p, :, cols]).astype(BF16)
             term = dot(n_t[p], d_before)
@@ -301,11 +303,19 @@
             @pl.when(p == 1)
             def _():
                 up_a[:, cols] = term.astype(BF16)
-                up_copy_a(c).start()
+                up_copy(c).start()
 
             @pl.when(p == 0)
             def _():
                 own_a[:, cols] = term
+
+        @pl.when(p == 0)
+        def _():
+            hidden_copy().wait_recv()
+            take_wait(1, 2)
+            ob[...] = (
+                dot(h_t[0], g_all[0].reshape(T, D)) + dot(hm_t[...], g_all[2].reshape(T, D))
+            ).astype(BF16)
 
     early = (k0 < S // 4).astype(jnp.int32)
     middle = (k0 == half - 1).astype(jnp.int32)
@@ -324,6 +334,11 @@
         def _():
             backward(p, k)
 
+        @pl.when((j >= 2) & (p == 0))
+        def _():
+            seed_copy().wait_recv()
+            share_start(1, 2)
+
         is1 = (j == 1).astype(jnp.int32)
         is2 = (j == 2).astype(jnp.int32)
         is3 = (j == 3).astype(jnp.int32)
@@ -341,11 +356,9 @@
             which = is2 + is3 * (middle - i)
             gradients(p0 + which * (1 - 2 * p0))
 
-    up_copy_b().wait_recv()
-    ob[...] = (own_b[...] + got_b[...].astype(F32)).astype(BF16)
-    for c in range(UNIT_CHUNKS):
-        cols = pl.ds(c * uw, uw)
-        up_copy_a(c).wait_recv()
+    for c in range(GRAD_CHUNKS):
+        cols = pl.ds(c * gw, gw)
+        up_copy(c).wait_recv()
         oa[:, cols] = (own_a[:, cols] + got_a[:, cols].astype(F32)).astype(BF16)
 
     for c in range(HOP_CHUNKS):
@@ -358,13 +371,40 @@
             hop(0, p1, c).wait_send()
             hop(1, p0, c).wait_send()
 
-    for kind in range(2):
-        for p in (p0, p1):
-            for o in range(1, DP):
-                share(kind, p, o).wait_send()
-    up_copy_b().wait_send()
-    for c in range(UNIT_CHUNKS):
-        up_copy_a(c).wait_send()
+    for kind, p in ((0, 0), (0, 1), (1, 0), (1, 1), (1, 2)):
+        for o in range(1, DP):
+            share(kind, p, o).wait_send()
+    hidden_copy().wait_send()
+    seed_copy().wait_send()
+    for c in range(GRAD_CHUNKS):
+        up_copy(c).wait_send()
+
+
+def widen_kernel(a_ref, b_ref, oa_ref, ob_ref):
+    oa_ref[0] = a_ref[...].astype(F32)
+    ob_ref[0] = b_ref[...].astype(F32)
+
+
+def widen(a, b):
+    parts = 2
+
+    def narrow(x):
+        return pl.BlockSpec((x.shape[0], x.shape[1] // parts), lambda i: (0, i))
+
+    def wide(x):
+        return pl.BlockSpec((1, x.shape[0], x.shape[1] // parts), lambda i: (0, 0, i))
+
+    return pl.pallas_call(
+        widen_kernel,
+        grid=(parts,),
+        out_shape=tuple(jax.ShapeDtypeStruct((1,) + x.shape, F32) for x in (a, b)),
+        in_specs=[narrow(a), narrow(b)],
+        out_specs=(wide(a), wide(b)),
+        compiler_params=pltpu.CompilerParams(vmem_limit_bytes=60 * 1024 * 1024),
+        cost_estimate=pl.CostEstimate(
+            flops=a.size + b.size, bytes_accessed=6 * (a.size + b.size), transcendentals=0
+        ),
+    )(a, b)
 
 
 def per_device(feed, proj_in, proj_out):
@@ -390,7 +430,7 @@
             vm((2, D, R), BF16),
             vm((2, R, D), BF16),
             vm((2, DP, M, D), BF16),
-            vm((2, DP, M, D), BF16),
+            vm((3, DP, M, D), BF16),
             vm((2, M, D), BF16),
             vm((2, M, D), BF16),
             vm((2, M, R), F32),
@@ -403,21 +443,21 @@
             vm((2, rb, T), BF16),
             vm((2, T, R), F32),
             vm((ra, R), BF16),
-            vm((rb, D), BF16),
             vm((ra, R), BF16),
-            vm((rb, D), BF16),
             vm((ra, R), F32),
-            vm((rb, D), F32),
+            vm((rb, T), BF16),
             vm((M, R), F32),
             vm((16, 128) if aligned else (D + R, T), BF16),
             dma((2, 2)),
             dma(()),
             dma((2, 2, HOP_CHUNKS)),
             dma((2, 2, HOP_CHUNKS)),
-            dma((2, 2, peers)),
-            dma((2, 2, peers)),
-            dma((1 + UNIT_CHUNKS,)),
-            dma((1 + UNIT_CHUNKS,)),
+            dma((2, 3, peers)),
+            dma((2, 3, peers)),
+            dma((GRAD_CHUNKS,)),
+            dma((GRAD_CHUNKS,)),
+            dma((2,)),
+            dma((2,)),
         ],
         compiler_params=pltpu.CompilerParams(
             collective_id=0, has_side_effects=True, vmem_limit_bytes=60 * 1024 * 1024
@@ -426,7 +466,7 @@
             flops=40 * M * D * R, bytes_accessed=16 * D * R, transcendentals=8 * T * R
         ),
     )(feed.reshape(2, M, D), proj_in, proj_out)
-    return grad_a.astype(F32)[None], grad_b.astype(F32)[None]
+    return widen(grad_a, grad_b)
 
 
 def solution(mesh):

time: 77.9 us -> 72.2 us (0.927)
  other arithmetic: 3.92 us -> 0 us
  Pallas kernels: 72.7 us -> 71.5 us
    broadcast_in_dim x2 -> x0, other arithmetic: 3.92 us -> none  [per_device(): return (grad_a.astype(F32)[None], grad_b.astype(F32)[None])]
    pallas_call x1, Pallas kernels: 72.7 us -> 69.3 us  [per_device(): pl.pallas_call(functools.partial(relay_kernel, S, DP, scale), out_shape=(...]
    pallas_call x0 -> x1, Pallas kernels: none -> 2.2 us  [widen(): pl.pallas_call(widen_kernel, grid=(parts,), out_shape=tuple((jax.ShapeDty...]
where the time goes in v4:
time: 72.2 us; the launch traced here: 72.1 us
  Pallas kernels  71.5 us (99%)
    pallas_call x1, Pallas kernels, per_device(): pl.pallas_call(functools.partial(relay_kernel, S, DP, scale), out_shape=(...  69.3 us
    pallas_call x1, Pallas kernels, widen(): pl.pallas_call(widen_kernel, grid=(parts,), out_shape=tuple((jax.ShapeDty...  2.2 us

profile of v4, /device:TPU:0, one launch (start us, length us, event | category | flops | bytes accessed | tf_op | source)
XLA Modules:
  0.0 72.1 jit_solution(6790438550108331815)
XLA Ops:
  0.6 69.3 %shard_map.50 = (bf16[128,1536]{1,0:T(8,128)(2,1)}, bf16[384,512]{1,0:T(8,128)(2,1)}) custom-call(bf16[2,64,512]{2,1,0:T(8,128)(2,1)} %bitcast.1, bf16[2,1,512,1536]{3,2,1,0:T(8,128)(2,1)} %win.1, bf16[2,1,1536,512]{3,2,1,0:T(8,128)(2,1)} %wout.1), custom_call_target="tpu_custom_call" | custom-call | flops 2013265920 | bytes 12582912 | tf_op jit(solution)/shard_map/pallas_call | solution.py:421
  69.9 2.2 %shard_map.51 = (f32[1,128,1536]{2,1,0:T(8,128)}, f32[1,384,512]{2,1,0:T(8,128)}) custom-call(bf16[128,1536]{1,0:T(8,128)(2,1)} %get-tuple-element.4.a_ref, bf16[384,512]{1,0:T(8,128)(2,1)} %get-tuple-element.5.b_ref), custom_call_target="tpu_custom_call" | custom-call | flops 393216 | bytes 2359296 | tf_op jit(solution)/shard_map/pallas_call | solution.py:397

commit v5 on v4

v5 whole, which is shorter than its diff:
```python
import functools

import jax
import jax.numpy as jnp
from jax import lax
from jax.experimental import pallas as pl
from jax.experimental.pallas import tpu as pltpu
from jax.sharding import PartitionSpec as P

MESH = pl.DeviceIdType.MESH
F32, BF16 = jnp.float32, jnp.bfloat16
HOP_CHUNKS = 2
UNIT_CHUNKS = 3
GRAD_CHUNKS = 3


def dot(a, b):
    return jnp.dot(a, b, preferred_element_type=F32)


def dot_nt(a, b):
    return lax.dot_general(a, b, (((1,), (1,)), ((), ())), preferred_element_type=F32)


def sigmoid(x):
    return 0.5 + 0.5 * jnp.tanh(0.5 * x)


def norm_factor(wide):
    return lax.rsqrt(jnp.mean(wide * wide, axis=-1, keepdims=True) + 1e-05)


def relay_kernel(
    S, DP, scale,
    feed, win, wout, oa, ob,
    wa, wb, h_all, g_all, h_out, g_out, pre_own, dsl_own, hid_own, dpre_own, u_own, r_own,
    n_t, h_t, dsl_all, up_a, got_a, own_a, own_b, hm_t, fin_a, fin_b, end_a, end_b,
    dh_own, full_t,
    load_sem, feed_sem, swap_send, swap_recv, hop_send, hop_recv, all_send, all_recv,
    up_send, up_recv, pair_send, pair_recv, fin_send, fin_recv,
):
    s, d = lax.axis_index("section"), lax.axis_index("dp")
    M, D = h_all.shape[2], h_all.shape[3]
    R = wa.shape[2]
    T = DP * M
    ra, rb = D // DP, R // DP
    last = S // 2 - 1
    p = lax.rem(s, 2)
    place = s // 2 + p * (last - 2 * (s // 2))
    mate = s + 1 - 2 * p
    stride = 2 * (1 - 2 * p)
    mirror = S - 1 - s
    cw, uw, gw = D // HOP_CHUNKS, R // UNIT_CHUNKS, R // GRAD_CHUNKS

    def unit_cols(c):
        return pl.ds(pl.multiple_of(c * uw, uw), uw)

    def load(i):
        src, dst = ((win, wa), (wout, wb))[i]
        return pltpu.make_async_copy(src.at[p, 0], dst.at[0], load_sem.at[i])

    def remote(src, dst, send_sem, recv_sem, section):
        return pltpu.make_async_remote_copy(
            src_ref=src,
            dst_ref=dst,
            send_sem=send_sem,
            recv_sem=recv_sem,
            device_id={"section": section},
            device_id_type=MESH,
        )

    def swap(i):
        src, dst = ((win, wa), (wout, wb))[i]
        return remote(src.at[1 - p, 0], dst.at[1], swap_send.at[i], swap_recv.at[i], mate)

    feed_copy = pltpu.make_async_copy(feed.at[p], h_all.at[0, d], feed_sem)

    @pl.when(place == 0)
    def _():
        feed_copy.start()

    load(0).start()
    load(1).start()

    barrier = pltpu.get_barrier_semaphore()
    for other in (mate, lax.rem(s + 2, S), lax.rem(s + S - 2, S), mirror):
        pl.semaphore_signal(barrier, inc=1, device_id={"section": other}, device_id_type=MESH)
    for o in range(1, DP):
        pl.semaphore_signal(
            barrier, inc=1, device_id={"dp": lax.rem(d + o, DP)}, device_id_type=MESH
        )
    pl.semaphore_wait(barrier, 4 + DP - 1)

    swap(0).start()
    swap(1).start()

    def hop(kind, c):
        cols = pl.ds(c * cw, cw)
        src, dst = ((h_out, h_all.at[0, d]), (g_out, g_all.at[1, d]))[kind]
        peer = s + stride if kind == 0 else s - stride
        return remote(
            src.at[:, cols], dst.at[:, cols], hop_send.at[kind, c], hop_recv.at[kind, c], peer
        )

    def share(kind, i, o, incoming=False):
        buf = (h_all, g_all)[kind]
        peer = lax.rem(d + (DP - o if incoming else o), DP)
        block = buf.at[i, peer if incoming else d]
        return pltpu.make_async_remote_copy(
            src_ref=block,
            dst_ref=block,
            send_sem=all_send.at[kind, i, o - 1],
            recv_sem=all_recv.at[kind, i, o - 1],
            device_id={"dp": peer},
            device_id_type=MESH,
        )

    def share_start(kind, i):
        for o in range(1, DP):
            share(kind, i, o).start()

    def take_wait(kind, i):
        for o in range(1, DP):
            share(kind, i, o, True).wait_recv()

    def up_copy(i, c):
        cols = pl.ds(c * gw, gw)
        return remote(
            up_a.at[i, :, cols], got_a.at[i, :, cols], up_send.at[i, c], up_recv.at[i, c], mirror
        )

    def hidden_copy(i):
        return remote(h_t.at[i], hm_t.at[i], pair_send.at[0, i], pair_recv.at[0, i], mirror)

    def seed_copy(i):
        return remote(
            g_all.at[i, d], g_all.at[2 + i, d], pair_send.at[1, i], pair_recv.at[1, i], mirror
        )

    def final_copy(i):
        src, dst = ((fin_a, end_a), (fin_b, end_b))[i]
        return remote(src, dst, fin_send.at[i], fin_recv.at[i], mate)

    def forward(i):
        steps = HOP_CHUNKS if i == 0 else 1
        width = D // steps
        squares = jnp.zeros((M, 1), F32)
        for c in range(steps):
            part = pl.ds(c * width, width)
            if i == 0:

                @pl.when(place > 0)
                def _():
                    hop(0, c).wait_recv()

            piece = h_all[i, d, :, part]
            wide = piece.astype(F32)
            squares += jnp.sum(wide * wide, axis=-1, keepdims=True)
            end = c == steps - 1
            if end:
                factor = lax.rsqrt(squares * (1.0 / D) + 1e-05)
            for u in range(UNIT_CHUNKS):
                cols = pl.ds(u * uw, uw)
                before = dot(piece, wa[i, part, cols])
                if c:
                    before += pre_own[i, :, cols]
                if end:
                    before *= factor
                    hid_own[:, cols] = (before * sigmoid(before)).astype(BF16)
                pre_own[i, :, cols] = before
        if i == 0:
            load(1).wait()
        else:
            swap(1).wait_recv()
        for c in range(HOP_CHUNKS):
            cols = pl.ds(c * cw, cw)
            old = h_all[i, d, :, cols].astype(F32)
            new = (old + dot(hid_own[...], wb[i, :, cols])).astype(BF16)
            if i == 0:
                h_all[1, d, :, cols] = new
            else:
                h_out[:, cols] = new

                @pl.when(place < last)
                def _():
                    hop(0, c).start()

    def forward_rest(i):
        share_start(0, i)
        wide = h_all[i, d].astype(F32)
        factor = norm_factor(wide)
        u_own[i] = wide * factor
        r_own[i] = jnp.broadcast_to(factor, (M, 128))
        for u in range(UNIT_CHUNKS):
            cols = pl.ds(u * uw, uw)
            before = pre_own[i, :, cols]
            sigma = sigmoid(before)
            dsl_own[i, :, cols] = sigma * (1.0 + before * (1.0 - sigma))

    def spread(i):
        share_start(1, i)

        @pl.when(p == 1)
        def _():
            seed_copy(i).start()

    def backward(i):
        steps = HOP_CHUNKS if i == 1 else 1
        width = D // steps
        total = jnp.zeros((M, 1), F32)
        for c in range(steps):
            part = pl.ds(c * width, width)
            if i == 1:

                @pl.when(place < last)
                def _():
                    hop(1, c).wait_recv()

                if c == steps - 1:
                    spread(1)

            piece = g_all[i, d, :, part]
            for u in range(UNIT_CHUNKS):
                cols = pl.ds(u * uw, uw)
                d_hidden = dot_nt(piece, wb[i, cols, part])
                if c:
                    d_hidden += dh_own[:, cols]
                if c < steps - 1:
                    dh_own[:, cols] = d_hidden
                else:
                    d_before = (d_hidden * dsl_own[i, :, cols]).astype(BF16)
                    dpre_own[:, cols] = d_before
                    total += jnp.sum(
                        d_before.astype(F32) * pre_own[i, :, cols], axis=-1, keepdims=True
                    )
        mean = total * (1.0 / D)
        factor = r_own[i, :, 0:1]
        for c in range(HOP_CHUNKS):
            cols = pl.ds(c * cw, cw)
            d_normed = dot_nt(dpre_own[...], wa[i, cols, :])
            out = g_all[i, d, :, cols].astype(F32) + factor * (
                d_normed - u_own[i, :, cols] * mean
            )
            if i == 1:
                g_all[0, d, :, cols] = out.astype(BF16)
            else:
                g_out[:, cols] = out.astype(BF16)
                hop(1, c).start()

    aligned = ra % 128 == 0 and rb % 128 == 0
    block = min(T, 256)

    def prepare(i):
        take_wait(0, i)

        def rows_step(b):
            per = block // M
            rows = pl.ds(pl.multiple_of(b * block, block), block)
            wide = h_all[i, pl.ds(b * per, per)].reshape(block, D).astype(F32)
            factor = norm_factor(wide)
            normed_wide = wide * factor
            normed = normed_wide.astype(BF16)
            if aligned:
                mine = h_all[
                    i, pl.ds(b * per, per), :, pl.ds(pl.multiple_of(d * ra, 128), ra)
                ].reshape(block, ra).astype(F32) * factor
                n_t[i, :, rows] = mine.T.astype(BF16)
                before = dot(normed, wa[i, :, pl.ds(pl.multiple_of(d * rb, 128), rb)])
                h_t[i, :, rows] = (before * sigmoid(before)).T.astype(BF16)
            else:
                full_t[0:D, rows] = normed_wide.T.astype(BF16)

            @pl.loop(0, UNIT_CHUNKS)
            def _(c):
                cols = unit_cols(c)
                before = dot(normed, wa[i, :, cols])
                sigma = sigmoid(before)
                dsl_all[i, rows, cols] = sigma * (1.0 + before * (1.0 - sigma))
                if not aligned:
                    full_t[pl.ds(pl.multiple_of(D + c * uw, 16), uw), rows] = (
                        (before * sigma).T.astype(BF16)
                    )

        if T == block:
            rows_step(0)
        else:
            pl.loop(0, T // block)(rows_step)
        if not aligned:
            n_t[i] = full_t[pl.ds(pl.multiple_of(d * ra, 16), ra), :]
            h_t[i] = full_t[pl.ds(pl.multiple_of(D + d * rb, 16), rb), :]

        @pl.when(p == 1)
        def _():
            hidden_copy(i).start()

    def gradients(i):
        take_wait(1, i)
        for c in range(GRAD_CHUNKS):
            cols = pl.ds(c * gw, gw)
            d_hidden = dot_nt(g_all[i].reshape(T, D), wb[i, cols, :])
            d_before = (d_hidden * dsl_all[i, :, cols]).astype(BF16)
            term = dot(n_t[i], d_before)

            @pl.when(p == 1)
            def _():
                up_a[i, :, cols] = term.astype(BF16)
                up_copy(i, c).start()

            @pl.when(p == 0)
            def _():
                own_a[i, :, cols] = term

        @pl.when(p == 0)
        def _():
            own_b[i] = dot(h_t[i], g_all[i].reshape(T, D))

    def finish(i, out_a, out_b):
        hidden_copy(i).wait_recv()
        take_wait(1, 2 + i)
        out_b[...] = (own_b[i] + dot(hm_t[i], g_all[2 + i].reshape(T, D))).astype(BF16)
        for c in range(GRAD_CHUNKS):
            cols = pl.ds(c * gw, gw)
            up_copy(i, c).wait_recv()
            out_a[:, cols] = (own_a[i, :, cols] + got_a[i, :, cols].astype(F32)).astype(BF16)

    load(0).wait()

    @pl.when(place == 0)
    def _():
        feed_copy.wait()

    forward(0)
    swap(0).wait_recv()
    forward(1)

    @pl.when(place == last)
    def _():
        g_all[1, d] = (scale * h_out[...].astype(F32)).astype(BF16)

    for i in range(2):
        forward_rest(i)

    @pl.when(place < last)
    def _():
        pl.loop(0, 2)(prepare)

    backward(1)

    @pl.when(p == 0)
    def _():
        seed_copy(1).wait_recv()
        share_start(1, 3)

    @pl.when(place > 0)
    def _():
        backward(0)

    spread(0)

    @pl.when(p == 0)
    def _():
        seed_copy(0).wait_recv()
        share_start(1, 2)

    @pl.when(place == last)
    def _():
        pl.loop(0, 2)(prepare)

    gradients(1)
    gradients(0)

    @pl.when(p == 0)
    def _():
        finish(1, fin_a, fin_b)
        final_copy(0).start()
        final_copy(1).start()
        finish(0, oa, ob)

    @pl.when(p == 1)
    def _():
        final_copy(0).wait_recv()
        oa[...] = end_a[...]
        final_copy(1).wait_recv()
        ob[...] = end_b[...]

    for i in range(2):
        swap(i).wait_send()

    for kind, sent in ((0, place < last), (1, place > 0)):

        @pl.when(sent)
        def _():
            for c in range(HOP_CHUNKS):
                hop(kind, c).wait_send()

        for i in range(2):
            for o in range(1, DP):
                share(kind, i, o).wait_send()

    @pl.when(p == 0)
    def _():
        for i in range(2):
            final_copy(i).wait_send()
            for o in range(1, DP):
                share(1, 2 + i, o).wait_send()

    @pl.when(p == 1)
    def _():
        for i in range(2):
            hidden_copy(i).wait_send()
            seed_copy(i).wait_send()
            for c in range(GRAD_CHUNKS):
                up_copy(i, c).wait_send()


def widen_kernel(a_ref, b_ref, oa_ref, ob_ref):
    oa_ref[0] = a_ref[...].astype(F32)
    ob_ref[0] = b_ref[...].astype(F32)


def widen(a, b):
    parts = 2

    def narrow(x):
        return pl.BlockSpec((x.shape[0], x.shape[1] // parts), lambda i: (0, i))

    def wide(x):
        return pl.BlockSpec((1, x.shape[0], x.shape[1] // parts), lambda i: (0, 0, i))

    return pl.pallas_call(
        widen_kernel,
        grid=(parts,),
        out_shape=tuple(jax.ShapeDtypeStruct((1,) + x.shape, F32) for x in (a, b)),
        in_specs=[narrow(a), narrow(b)],
        out_specs=(wide(a), wide(b)),
        compiler_params=pltpu.CompilerParams(vmem_limit_bytes=60 * 1024 * 1024),
        cost_estimate=pl.CostEstimate(
            flops=a.size + b.size, bytes_accessed=6 * (a.size + b.size), transcendentals=0
        ),
    )(a, b)


def per_device(feed, proj_in, proj_out):
    S, DP = lax.axis_size("section"), lax.axis_size("dp")
    micro, rows, D = feed.shape[1:]
    R = proj_in.shape[3]
    M, T = micro * rows, micro * rows * DP
    ra, rb = D // DP, R // DP
    scale = 8.0 / T
    aligned = ra % 128 == 0 and rb % 128 == 0
    vm = pltpu.VMEM
    dma = pltpu.SemaphoreType.DMA
    peers = max(DP - 1, 1)
    grad_a, grad_b = pl.pallas_call(
        functools.partial(relay_kernel, S, DP, scale),
        out_shape=(
            jax.ShapeDtypeStruct((ra, R), BF16),
            jax.ShapeDtypeStruct((rb, D), BF16),
        ),
        in_specs=[pl.BlockSpec(memory_space=pltpu.HBM)] * 3,
        out_specs=(pl.BlockSpec(memory_space=pltpu.VMEM),) * 2,
        scratch_shapes=[
            vm((2, D, R), BF16),
            vm((2, R, D), BF16),
            vm((2, DP, M, D), BF16),
            vm((4, DP, M, D), BF16),
            vm((M, D), BF16),
            vm((M, D), BF16),
            vm((2, M, R), F32),
            vm((2, M, R), F32),
            vm((M, R), BF16),
            vm((M, R), BF16),
            vm((2, M, D), F32),
            vm((2, M, 128), F32),
            vm((2, ra, T), BF16),
            vm((2, rb, T), BF16),
            vm((2, T, R), F32),
            vm((2, ra, R), BF16),
            vm((2, ra, R), BF16),
            vm((2, ra, R), F32),
            vm((2, rb, D), F32),
            vm((2, rb, T), BF16),
            vm((ra, R), BF16),
            vm((rb, D), BF16),
            vm((ra, R), BF16),
            vm((rb, D), BF16),
            vm((M, R), F32),
            vm((16, 128) if aligned else (D + R, T), BF16),
            dma((2,)),
            dma(()),
            dma((2,)),
            dma((2,)),
            dma((2, HOP_CHUNKS)),
            dma((2, HOP_CHUNKS)),
            dma((2, 4, peers)),
            dma((2, 4, peers)),
            dma((2, GRAD_CHUNKS)),
            dma((2, GRAD_CHUNKS)),
            dma((2, 2)),
            dma((2, 2)),
            dma((2,)),
            dma((2,)),
        ],
        compiler_params=pltpu.CompilerParams(
            collective_id=0, has_side_effects=True, vmem_limit_bytes=60 * 1024 * 1024
        ),
        cost_estimate=pl.CostEstimate(
            flops=40 * M * D * R, bytes_accessed=16 * D * R, transcendentals=8 * T * R
        ),
    )(feed.reshape(2, M, D), proj_in, proj_out)
    return widen(grad_a, grad_b)


def solution(mesh):
    in_specs = (
        P(None, None, "dp", None),
        P(None, "section", None, None),
        P(None, "section", None, None),
    )
    out_specs = (P("section", "dp", None), P("section", "dp", None))
    return jax.shard_map(
        per_device, mesh=mesh, in_specs=in_specs, out_specs=out_specs, check_vma=False
    )
```

time: 72.2 us -> 66.7 us (0.924)
  the two profiles are of different devices: /device:TPU:0 before, /device:TPU:25 now
where the time goes in v5:
time: 66.7 us; the launch traced here: 66.6 us
  Pallas kernels  65.9 us (99%)
    pallas_call x1, Pallas kernels, per_device(): pl.pallas_call(functools.partial(relay_kernel, S, DP, scale), out_shape=(...  63.7 us
    pallas_call x1, Pallas kernels, widen(): pl.pallas_call(widen_kernel, grid=(parts,), out_shape=tuple((jax.ShapeDty...  2.2 us

profile of v5, /device:TPU:25, one launch (start us, length us, event | category | flops | bytes accessed | tf_op | source)
XLA Modules:
  0.0 66.6 jit_solution(13803739828916700006)
XLA Ops:
  0.6 63.7 %shard_map.50 = (bf16[128,1536]{1,0:T(8,128)(2,1)}, bf16[384,512]{1,0:T(8,128)(2,1)}) custom-call(bf16[2,64,512]{2,1,0:T(8,128)(2,1)} %bitcast.1, bf16[2,1,512,1536]{3,2,1,0:T(8,128)(2,1)} %win.1, bf16[2,1,1536,512]{3,2,1,0:T(8,128)(2,1)} %wout.1), custom_call_target="tpu_custom_call" | custom-call | flops 2013265920 | bytes 12582912 | tf_op jit(solution)/shard_map/pallas_call | solution.py:454
  64.4 2.2 %shard_map.51 = (f32[1,128,1536]{2,1,0:T(8,128)}, f32[1,384,512]{2,1,0:T(8,128)}) custom-call(bf16[128,1536]{1,0:T(8,128)(2,1)} %get-tuple-element.4.a_ref, bf16[384,512]{1,0:T(8,128)(2,1)} %get-tuple-element.5.b_ref), custom_call_target="tpu_custom_call" | custom-call | flops 393216 | bytes 2359296 | tf_op jit(solution)/shard_map/pallas_call | solution.py:430

commit v6 on v5

--- a/solution.py
+++ b/solution.py
@@ -18,10 +18,6 @@
     return jnp.dot(a, b, preferred_element_type=F32)
 
 
-def dot_nt(a, b):
-    return lax.dot_general(a, b, (((1,), (1,)), ((), ())), preferred_element_type=F32)
-
-
 def sigmoid(x):
     return 0.5 + 0.5 * jnp.tanh(0.5 * x)
 
@@ -33,7 +29,7 @@
 def relay_kernel(
     S, DP, scale,
     feed, win, wout, oa, ob,
-    wa, wb, h_all, g_all, h_out, g_out, pre_own, dsl_own, hid_own, dpre_own, u_own, r_own,
+    wa, wb, wat, wbt, h_all, g_all, h_out, g_out, pre_own, dsl_own, hid_own, dpre_own, u_own, r_own,
     n_t, h_t, dsl_all, up_a, got_a, own_a, own_b, hm_t, fin_a, fin_b, end_a, end_b,
     dh_own, full_t,
     load_sem, feed_sem, swap_send, swap_recv, hop_send, hop_recv, all_send, all_recv,
@@ -168,10 +164,14 @@
                     before *= factor
                     hid_own[:, cols] = (before * sigmoid(before)).astype(BF16)
                 pre_own[i, :, cols] = before
-        if i == 0:
-            load(1).wait()
-        else:
-            swap(1).wait_recv()
+
+        @pl.when(place < last)
+        def _():
+            if i == 0:
+                load(1).wait()
+            else:
+                swap(1).wait_recv()
+
         for c in range(HOP_CHUNKS):
             cols = pl.ds(c * cw, cw)
             old = h_all[i, d, :, cols].astype(F32)
@@ -222,7 +222,7 @@
             piece = g_all[i, d, :, part]
             for u in range(UNIT_CHUNKS):
                 cols = pl.ds(u * uw, uw)
-                d_hidden = dot_nt(piece, wb[i, cols, part])
+                d_hidden = dot(piece, wbt[i, part, cols])
                 if c:
                     d_hidden += dh_own[:, cols]
                 if c < steps - 1:
@@ -237,7 +237,7 @@
         factor = r_own[i, :, 0:1]
         for c in range(HOP_CHUNKS):
             cols = pl.ds(c * cw, cw)
-            d_normed = dot_nt(dpre_own[...], wa[i, cols, :])
+            d_normed = dot(dpre_own[...], wat[i, :, cols])
             out = g_all[i, d, :, cols].astype(F32) + factor * (
                 d_normed - u_own[i, :, cols] * mean
             )
@@ -297,7 +297,7 @@
         take_wait(1, i)
         for c in range(GRAD_CHUNKS):
             cols = pl.ds(c * gw, gw)
-            d_hidden = dot_nt(g_all[i].reshape(T, D), wb[i, cols, :])
+            d_hidden = dot(g_all[i].reshape(T, D), wbt[i, :, cols])
             d_before = (d_hidden * dsl_all[i, :, cols]).astype(BF16)
             term = dot(n_t[i], d_before)
 
@@ -323,14 +323,34 @@
             up_copy(i, c).wait_recv()
             out_a[:, cols] = (own_a[i, :, cols] + got_a[i, :, cols].astype(F32)).astype(BF16)
 
+    def turn_weights():
+        @pl.loop(0, 2)
+        def _(i):
+            @pl.loop(0, UNIT_CHUNKS)
+            def _(c):
+                cols = unit_cols(c)
+                wbt[i, :, cols] = wb[i, cols, :].T
+                wat[i, cols, :] = wa[i, :, cols].T
+
     load(0).wait()
 
+    @pl.when(place == last)
+    def _():
+        load(1).wait()
+        for i in range(2):
+            swap(i).wait_recv()
+        turn_weights()
+
     @pl.when(place == 0)
     def _():
         feed_copy.wait()
 
     forward(0)
-    swap(0).wait_recv()
+
+    @pl.when(place < last)
+    def _():
+        swap(0).wait_recv()
+
     forward(1)
 
     @pl.when(place == last)
@@ -342,6 +362,7 @@
 
     @pl.when(place < last)
     def _():
+        turn_weights()
         pl.loop(0, 2)(prepare)
 
     backward(1)
@@ -462,6 +483,8 @@
         scratch_shapes=[
             vm((2, D, R), BF16),
             vm((2, R, D), BF16),
+            vm((2, R, D), BF16),
+            vm((2, D, R), BF16),
             vm((2, DP, M, D), BF16),
             vm((4, DP, M, D), BF16),
             vm((M, D), BF16),

time: 66.7 us -> 65.9 us (0.988)
  Pallas kernels: 65.9 us -> 65.1 us
    pallas_call x1, Pallas kernels: 63.7 us -> 62.9 us  [per_device(): pl.pallas_call(functools.partial(relay_kernel, S, DP, scale), out_shape=(...]
where the time goes in v6:
time: 65.9 us; the launch traced here: 65.8 us
  Pallas kernels  65.1 us (99%)
    pallas_call x1, Pallas kernels, per_device(): pl.pallas_call(functools.partial(relay_kernel, S, DP, scale), out_shape=(...  62.9 us
    pallas_call x1, Pallas kernels, widen(): pl.pallas_call(widen_kernel, grid=(parts,), out_shape=tuple((jax.ShapeDty...  2.2 us

profile of v6, /device:TPU:25, one launch (start us, length us, event | category | flops | bytes accessed | tf_op | source)
XLA Modules:
  0.0 65.8 jit_solution(91816356797160928)
XLA Ops:
  0.6 62.9 %shard_map.50 = (bf16[128,1536]{1,0:T(8,128)(2,1)}, bf16[384,512]{1,0:T(8,128)(2,1)}) custom-call(bf16[2,64,512]{2,1,0:T(8,128)(2,1)} %bitcast.1, bf16[2,1,512,1536]{3,2,1,0:T(8,128)(2,1)} %win.1, bf16[2,1,1536,512]{3,2,1,0:T(8,128)(2,1)} %wout.1), custom_call_target="tpu_custom_call" | custom-call | flops 2013265920 | bytes 12582912 | tf_op jit(solution)/shard_map/pallas_call | solution.py:475
  63.6 2.2 %shard_map.51 = (f32[1,128,1536]{2,1,0:T(8,128)}, f32[1,384,512]{2,1,0:T(8,128)}) custom-call(bf16[128,1536]{1,0:T(8,128)(2,1)} %get-tuple-element.4.a_ref, bf16[384,512]{1,0:T(8,128)(2,1)} %get-tuple-element.5.b_ref), custom_call_target="tpu_custom_call" | custom-call | flops 393216 | bytes 2359296 | tf_op jit(solution)/shard_map/pallas_call | solution.py:451

commit v7 on v6

--- a/solution.py
+++ b/solution.py
@@ -12,6 +12,7 @@
 HOP_CHUNKS = 2
 UNIT_CHUNKS = 3
 GRAD_CHUNKS = 3
+SWAP_BLOCKS = 4
 
 
 def dot(a, b):
@@ -65,9 +66,16 @@
             device_id_type=MESH,
         )
 
-    def swap(i):
+    def swap(i, b):
         src, dst = ((win, wa), (wout, wb))[i]
-        return remote(src.at[1 - p, 0], dst.at[1], swap_send.at[i], swap_recv.at[i], mate)
+        rows = pl.ds(b * (dst.shape[1] // SWAP_BLOCKS), dst.shape[1] // SWAP_BLOCKS)
+        return remote(
+            src.at[1 - p, 0, rows], dst.at[1, rows], swap_send.at[i, b], swap_recv.at[i, b], mate
+        )
+
+    def swap_wait(i):
+        for b in range(SWAP_BLOCKS):
+            swap(i, b).wait_recv()
 
     feed_copy = pltpu.make_async_copy(feed.at[p], h_all.at[0, d], feed_sem)
 
@@ -87,8 +95,9 @@
         )
     pl.semaphore_wait(barrier, 4 + DP - 1)
 
-    swap(0).start()
-    swap(1).start()
+    for i in range(2):
+        for b in range(SWAP_BLOCKS):
+            swap(i, b).start()
 
     def hop(kind, c):
         cols = pl.ds(c * cw, cw)
@@ -170,7 +179,7 @@
             if i == 0:
                 load(1).wait()
             else:
-                swap(1).wait_recv()
+                swap_wait(1)
 
         for c in range(HOP_CHUNKS):
             cols = pl.ds(c * cw, cw)
@@ -338,7 +347,7 @@
     def _():
         load(1).wait()
         for i in range(2):
-            swap(i).wait_recv()
+            swap_wait(i)
         turn_weights()
 
     @pl.when(place == 0)
@@ -349,7 +358,7 @@
 
     @pl.when(place < last)
     def _():
-        swap(0).wait_recv()
+        swap_wait(0)
 
     forward(1)
 
@@ -367,21 +376,17 @@
 
     backward(1)
 
+    @pl.when(place > 0)
+    def _():
+        backward(0)
+
+    spread(0)
+
     @pl.when(p == 0)
     def _():
-        seed_copy(1).wait_recv()
-        share_start(1, 3)
-
-    @pl.when(place > 0)
-    def _():
-        backward(0)
-
-    spread(0)
-
-    @pl.when(p == 0)
-    def _():
-        seed_copy(0).wait_recv()
-        share_start(1, 2)
+        for i in (1, 0):
+            seed_copy(i).wait_recv()
+            share_start(1, 2 + i)
 
     @pl.when(place == last)
     def _():
@@ -405,7 +410,8 @@
         ob[...] = end_b[...]
 
     for i in range(2):
-        swap(i).wait_send()
+        for b in range(SWAP_BLOCKS):
+            swap(i, b).wait_send()
 
     for kind, sent in ((0, place < last), (1, place > 0)):
 
@@ -511,8 +517,8 @@
             vm((16, 128) if aligned else (D + R, T), BF16),
             dma((2,)),
             dma(()),
-            dma((2,)),
-            dma((2,)),
+            dma((2, SWAP_BLOCKS)),
+            dma((2, SWAP_BLOCKS)),
             dma((2, HOP_CHUNKS)),
             dma((2, HOP_CHUNKS)),
             dma((2, 4, peers)),

time: 65.9 us -> 62.1 us (0.942)
  the two profiles are of different devices: /device:TPU:25 before, /device:TPU:0 now
where the time goes in v7:
time: 62.1 us; the launch traced here: 61.3 us
  Pallas kernels  60.7 us (98%)
  between operations  0.64 us (1%)
    pallas_call x1, Pallas kernels, per_device(): pl.pallas_call(functools.partial(relay_kernel, S, DP, scale), out_shape=(...  58.5 us
    pallas_call x1, Pallas kernels, widen(): pl.pallas_call(widen_kernel, grid=(parts,), out_shape=tuple((jax.ShapeDty...  2.2 us

profile of v7, /device:TPU:0, one launch (start us, length us, event | category | flops | bytes accessed | tf_op | source)
XLA Modules:
  0.0 61.3 jit_solution(7768913208169283875)
XLA Ops:
  0.6 58.5 %shard_map.50 = (bf16[128,1536]{1,0:T(8,128)(2,1)}, bf16[384,512]{1,0:T(8,128)(2,1)}) custom-call(bf16[2,64,512]{2,1,0:T(8,128)(2,1)} %bitcast.1, bf16[2,1,512,1536]{3,2,1,0:T(8,128)(2,1)} %win.1, bf16[2,1,1536,512]{3,2,1,0:T(8,128)(2,1)} %wout.1), custom_call_target="tpu_custom_call" | custom-call | flops 2013265920 | bytes 12582912 | tf_op jit(solution)/shard_map/pallas_call | solution.py:481
  59.1 2.2 %shard_map.51 = (f32[1,128,1536]{2,1,0:T(8,128)}, f32[1,384,512]{2,1,0:T(8,128)}) custom-call(bf16[128,1536]{1,0:T(8,128)(2,1)} %get-tuple-element.4.a_ref, bf16[384,512]{1,0:T(8,128)(2,1)} %get-tuple-element.5.b_ref), custom_call_target="tpu_custom_call" | custom-call | flops 393216 | bytes 2359296 | tf_op jit(solution)/shard_map/pallas_call | solution.py:457
